TPU v7x, 128 devices: a whole 4x4x4 slice. The times are simulated.
128 devices in a mesh: step: 8 (over y, core), seq: 16 (over z, x).
Axes of the slice: x: 4, y: 4, z: 4, core: 2. Of those that a mesh axis runs over, the one named last changes fastest.
Arguments:
- iterate: float32 [8, 4096, 2048], P('step', 'seq'), may hold values from -6 to 6
- query_key_value_weight: bfloat16 [2048, 16, 384], P(None, 'seq'), may hold values from -0.125 to 0.125
- modulation_down_weight: bfloat16 [2048, 256], replicated, may hold values from -0.125 to 0.125
- modulation_up_weight: bfloat16 [256, 6144], replicated, may hold values from -0.375 to 0.375
- action_embedding_matrix: bfloat16 [512, 2048], replicated, may hold values from -12 to 12
- action_token_index: int32 [12], replicated, may hold values from 0 to 511
- sched: int32 [36], replicated, may hold values from 55 to 1000, as said below
- window: int32 [9], replicated, may hold values from 0 to 35, as said below
Outputs:
- new_states: float32 [8, 4096, 2048], P('step', 'seq')
- velocity: float32 [8, 4096, 2048], P('step', 'seq')
Inputs may be any that keep to these rules, and one draw needn't show every extreme that they name: `sched`: strictly decreasing; entry 0 is 1000 and neighbouring entries differ by 5 to 27. `window`: strictly increasing; the first entry is 0 and the last is 35.
All inputs are finite; a program needn't handle non-finite values.
Results may differ from a plain program's by a relative error of at most 0.011.
Values may be sent and summed in bfloat16 or wider, within the bound.
A program may use at most 128 MiB of HBM per device.

v0:
```python
import math

import jax
import jax.numpy as jnp
from jax import lax
from jax.sharding import PartitionSpec as P


def entering(x, axis, join, neutral):
    place = lax.axis_index(axis)
    gathered = lax.all_gather(x.astype(jnp.bfloat16), axis)
    state = jnp.zeros_like(x) + jnp.asarray(neutral, x.dtype)

    def one(step, state):
        return join(state, lax.dynamic_index_in_dim(gathered, step, 0, False).astype(x.dtype))

    return lax.fori_loop(0, place, one, state)


def embed_time(timestep_markers, hidden_width):
    half = hidden_width // 2
    freqs = jnp.exp(-math.log(10000.0) * jnp.arange(half, dtype=jnp.float32) / half)
    angles = timestep_markers[:, None] * freqs[None, :]
    return jnp.concatenate([jnp.cos(angles), jnp.sin(angles)], axis=1)


def apply_modulation(
    timestep_markers,
    action_embedding_matrix,
    action_token_index,
    modulation_down_weight,
    modulation_up_weight,
):
    hidden_width = action_embedding_matrix.shape[1]
    onehot = (
        action_token_index[:, None]
        == jnp.arange(action_embedding_matrix.shape[0], dtype=jnp.int32)[None, :]
    ).astype(jnp.bfloat16)
    action_mean = jnp.mean(
        jnp.dot(onehot, action_embedding_matrix, preferred_element_type=jnp.float32), axis=0
    )
    conditioning_vector = jax.nn.silu(
        embed_time(timestep_markers, hidden_width) + action_mean[None, :]
    ).astype(jnp.bfloat16)
    reduced_rank_update = jnp.dot(
        conditioning_vector, modulation_down_weight, preferred_element_type=jnp.float32
    ).astype(jnp.bfloat16)
    return jnp.dot(
        reduced_rank_update, modulation_up_weight, preferred_element_type=jnp.float32
    ).reshape(timestep_markers.shape[0], 3, hidden_width)


def norm_shift(state, shift, scale):
    spread = jnp.sqrt(jnp.mean(state * state, axis=-1, keepdims=True) + 1e-06)
    return (state / spread * (1.0 + scale[None, :]) + shift[None, :]).astype(jnp.bfloat16)


def normalize_heads(projected):
    head_dim = projected.shape[-1] // 3
    queries = projected[..., :head_dim]
    keys = projected[..., head_dim : 2 * head_dim]
    values = projected[..., 2 * head_dim :]
    queries = queries / jnp.sqrt(jnp.mean(queries * queries, axis=-1, keepdims=True) + 1e-06)
    keys = keys / jnp.sqrt(jnp.mean(keys * keys, axis=-1, keepdims=True) + 1e-06)
    return jnp.concatenate([queries, keys, values], axis=-1).astype(jnp.bfloat16)


def attend_heads(packed):
    count = packed.shape[0]
    head_dim = packed.shape[2] // 3
    block = math.gcd(count, 512)
    factor = 2.5 / math.sqrt(head_dim)

    def one_head(head):
        keys = head[:, head_dim : 2 * head_dim]
        values = head[:, 2 * head_dim :]
        queries = head[:, :head_dim].reshape(count // block, block, head_dim)

        def one_block(query_rows):
            scores = (
                jnp.einsum("qd,kd->qk", query_rows, keys, preferred_element_type=jnp.float32)
                * factor
            )
            weights = jnp.exp(scores)
            total = jnp.sum(weights, axis=1, keepdims=True)
            mixed = (
                jnp.dot(weights.astype(jnp.bfloat16), values, preferred_element_type=jnp.float32)
                / total
            )
            return mixed.astype(jnp.bfloat16)

        return lax.map(one_block, queries).reshape(count, head_dim)

    result = lax.map(one_head, jnp.moveaxis(packed, 1, 0))
    return jnp.transpose(result, (1, 0, 2))


def attend_group(group):
    return attend_heads(group[:, 0])[:, None]


def add_terms(earlier, later):
    return earlier + later


def on_device(
    iterate,
    query_key_value_weight,
    modulation_down_weight,
    modulation_up_weight,
    action_embedding_matrix,
    action_token_index,
    sched,
    window,
):
    step_count = iterate.shape[0]
    tok_rows = iterate.shape[1]
    hidden_width = iterate.shape[2]
    heads_local = query_key_value_weight.shape[1]
    head_dim = query_key_value_weight.shape[2] // 3
    groups = lax.axis_size("seq")
    first_step = lax.axis_index("step") * step_count
    position = first_step + jnp.arange(step_count + 1, dtype=jnp.int32)
    chosen = jnp.sum(
        jnp.where(
            position[:, None] == jnp.arange(window.shape[0], dtype=jnp.int32)[None, :],
            window[None, :],
            0,
        ),
        axis=1,
    )
    stamps_int = jnp.sum(
        jnp.where(
            chosen[:, None] == jnp.arange(sched.shape[0], dtype=jnp.int32)[None, :],
            sched[None, :],
            0,
        ),
        axis=1,
    )
    timestep_markers = stamps_int.astype(jnp.float32)
    sigma = timestep_markers / 1000.0
    delta = sigma[1:] - sigma[:-1]
    modulation_factors = apply_modulation(
        timestep_markers[:-1],
        action_embedding_matrix,
        action_token_index,
        modulation_down_weight,
        modulation_up_weight,
    )
    normed = norm_shift(iterate[0], modulation_factors[0, 0], modulation_factors[0, 1])
    projected = jnp.einsum(
        "td,dhe->the",
        normed,
        lax.all_gather(query_key_value_weight, "seq", axis=1, tiled=True),
        preferred_element_type=jnp.float32,
    )
    packed = normalize_heads(projected)
    grouped = packed.reshape(tok_rows, groups, heads_local, 3 * head_dim)
    attended = attend_group(lax.all_to_all(grouped, "seq", split_axis=1, concat_axis=0, tiled=True))
    attended = attended.reshape(attended.shape[0], heads_local, head_dim)
    mixed = lax.all_to_all(attended, "seq", split_axis=0, concat_axis=1, tiled=True)
    mixed = mixed.reshape(tok_rows, hidden_width).astype(jnp.float32)
    drifts = [modulation_factors[0, 2][None, :] * mixed]
    velocity = jnp.stack(drifts, axis=0)
    terms = delta[:, None, None] * velocity
    starting = first_step + jnp.arange(step_count, dtype=jnp.int32) == 0
    terms = terms + jnp.where(starting[:, None, None], iterate, 0.0)
    local_sums = jnp.cumsum(terms, axis=0)
    earlier = entering(local_sums[-1], "step", add_terms, jnp.zeros_like(local_sums[-1]))
    new_states = local_sums + earlier[None]
    return (new_states, velocity)


def solution(mesh):
    placed = (P("step", "seq", None), P(None, "seq", None), P(), P(), P(), P(), P(), P())
    return jax.shard_map(
        on_device,
        mesh=mesh,
        in_specs=placed,
        out_specs=(P("step", "seq", None), P("step", "seq", None)),
        check_vma=False,
    )
```

profile of v0, /device:TPU:25, one launch (start us, length us, event | category | flops | bytes accessed | tf_op | source)
XLA Modules:
  0.0 379.1 jit_solution(15180414385945670431)
XLA Ops:
  7.2 0.7 all-gather.3.cloned.1.call-update
  7.9 1.0 fusion.39
  9.0 0.8 fusion.40
  9.8 0.1 fusion.37
  9.9 1.1 convolution_reduce_fusion
  11.0 0.2 fusion.44
  11.3 4.8 %copy.37 = bf16[256,6144]{0,1:T(8,128)(2,1)} copy(bf16[256,6144]{1,0:T(8,128)(2,1)} %param.15) | data formatting | bytes 6291456 | tf_op args[3]
  16.2 0.2 fusion.22
  16.4 2.8 fusion.45
  19.2 147.4 %all-gather.3.cloned.1.call-done = bf16[2048,16,384]{2,0,1:T(8,128)(2,1)} async-done(((bf16[2048,1,384]{2,0,1:T(8,128)(2,1)}), bf16[2048,16,384]{2,0,1:T(8,128)(2,1)}) %all-gather.3.cloned.1.call-update) | async-done | bytes 25165840 | tf_op jit(solution)/shard_map/all_gather | solution.py:154
  166.6 11.6 %fusion.27 = f32[256,16,384]{2,0,1:T(8,128)S(1)} fusion(bf16[2048,16,384]{2,0,1:T(8,128)(2,1)} %all-gather.3.cloned.1.call-done, f32[1,256,2048]{2,1,0:T(8,128)S(1)} %copy-done.4, f32[2048]{0:T(1024)S(1)} %bitcast.95, f32[2048]{0:T(1024)S(1)} %bitcast.94, f32[256]{0:T(256)S(1)} %add_sqrt_fusion.2), kind=kOutput, calls=%fused_computation.33 | convolution fusion | flops 6444548096 | bytes 33571840 | tf_op jit(solution)/shard_map/td,dhe->the/dot_general | solution.py:151
  178.3 1.2 multiply_reduce_fusion.1
  179.4 0.2 fusion.26
  179.7 1.5 fusion.32
  181.1 2.2 maximum_bitcast_fusion
  183.3 5.1 %all-to-all-start = ((bf16[256,16,1,384]{3,0,2,1:T(8,128)(2,1)}), bf16[256,16,1,384]{3,0,2,1:T(8,128)(2,1)}, u32[]{:S(2)}, u32[]{:S(2)}) async-start(bf16[256,16,1,384]{3,0,2,1:T(8,128)(2,1)} %maximum_bitcast_fusion), calls=%async_computation | async-start | bytes 6291456 | tf_op jit(solution)/shard_map/all_to_all | solution.py:159
  188.4 46.7 %all-to-all-done = bf16[256,16,1,384]{3,0,2,1:T(8,128)(2,1)} async-done(((bf16[256,16,1,384]{3,0,2,1:T(8,128)(2,1)}), bf16[256,16,1,384]{3,0,2,1:T(8,128)(2,1)}, u32[]{:S(2)}, u32[]{:S(2)}) %all-to-all-start) | async-done | bytes 3145760 | tf_op jit(solution)/shard_map/all_to_all | solution.py:159
  235.1 2.1 fusion.41
  237.1 27.3 %while.27 = (s32[]{:T(128)}, bf16[8,512,128]{2,1,0:T(8,128)(2,1)}, bf16[8,512,128]{2,1,0:T(8,128)(2,1)S(1)}, bf16[4096,128]{1,0:T(8,128)(2,1)S(1)}, bf16[4096,128]{1,0:T(8,128)(2,1)S(1)}, /*index=5*/s32[]{:T(128)}) while((s32[]{:T(128)}, bf16[8,512,128]{2,1,0:T(8,128)(2,1)}, bf16[8,512,128]{2,1,0:T(8,128)(2,1)S(1)}, ...), condition=%wide.region_8.9_spmd, body=%wide.region_6.8_spmd.sunk | while | flops 1082260992 | bytes 19141192 | solution.py:92
  237.1 1.4 fusion.62
  238.6 2.0 fusion.63
  240.5 1.4 fusion.62
  242.0 2.0 fusion.63
  244.0 1.4 fusion.62
  245.4 2.0 fusion.63
  247.4 1.4 fusion.62
  248.8 2.0 fusion.63
  250.8 1.4 fusion.62
  252.2 2.0 fusion.63
  254.2 1.4 fusion.62
  255.6 2.0 fusion.63
  257.6 1.4 fusion.62
  259.1 2.0 fusion.63
  261.0 1.4 fusion.62
  262.5 2.0 fusion.63
  264.5 0.5 broadcast.163
  265.0 2.7 reduce
  267.6 1.1 reshape.238
  268.7 4.1 %all-to-all-start.1 = ((bf16[16,2,16384]{2,1,0:T(2,128)(2,1)}), bf16[16,2,16384]{2,1,0:T(2,128)(2,1)S(1)}, u32[]{:S(2)}, u32[]{:S(2)}) async-start(bf16[16,2,16384]{2,1,0:T(2,128)(2,1)} %reshape.238), calls=%async_computation.1 | async-start | bytes 2097152 | tf_op jit(solution)/shard_map/all_to_all | solution.py:161
  272.9 0.2 all-gather.5.cloned.1.call-start
  273.1 1.9 copy.42
  275.0 0.7 fusion.43
  277.0 10.8 %all-to-all-done.1 = bf16[16,2,16384]{2,1,0:T(2,128)(2,1)S(1)} async-done(((bf16[16,2,16384]{2,1,0:T(2,128)(2,1)}), bf16[16,2,16384]{2,1,0:T(2,128)(2,1)S(1)}, u32[]{:S(2)}, u32[]{:S(2)}) %all-to-all-start.1) | async-done | bytes 1048608 | tf_op jit(solution)/shard_map/all_to_all | solution.py:161
  287.8 3.4 reshape.239
  291.3 1.7 copy.40
  293.0 1.5 convert_bitcast_fusion
  294.5 2.9 copy.41
  297.4 3.3 fusion.34
  300.7 1.4 copy.43
  302.1 0.5 copy-done.3
  302.6 1.8 copy.46
  304.4 46.4 %all-gather.5.cloned.1.call-done = bf16[8,256,2048]{2,1,0:T(8,128)(2,1)} async-done(((bf16[1,256,2048]{2,1,0:T(8,128)(2,1)}), bf16[8,256,2048]{2,1,0:T(8,128)(2,1)}) %all-gather.5.cloned.1.call-update) | async-done | bytes 8388624 | tf_op jit(solution)/shard_map/all_gather | solution.py:11
  350.8 0.2 broadcast_in_dim.73
  351.0 12.4 %while.28 = (s32[]{:T(128)}, f32[256,2048]{1,0:T(8,128)S(1)}, s32[]{:T(128)}, bf16[8,256,2048]{2,1,0:T(8,128)(2,1)}, s32[]{:T(128)}, /*index=5*/s32[]{:T(128)}, s32[]{:T(128)}) while((s32[]{:T(128)}, f32[256,2048]{1,0:T(8,128)S(1)}, s32[]{:T(128)}, bf16[8,256,2048]{2,1,0:T(8,128)(2,1)}, s32[]{:T(128)}, /*index=5*/s32[]{:T(128)}, ...), condition=%wide.region_10.11_spmd, body=%wide.region_9.10_spmd.sunk | while | flops 1048581 | bytes 5242995 | solution.py:17
  351.1 1.7 convert_add_fusion.2
  352.8 1.7 convert_add_fusion.2
  354.6 1.7 convert_add_fusion.2
  356.4 1.7 convert_add_fusion.2
  358.2 1.7 convert_add_fusion.2
  359.9 1.7 convert_add_fusion.2
  361.7 1.7 convert_add_fusion.2
  363.5 1.8 copy.44
  365.3 4.1 %bitcast_add_fusion = f32[1,256,2048]{1,2,0:T(8,128)} fusion(f32[256,2048]{0,1:T(8,128)} %copy.44, f32[1,256,2048]{1,2,0:T(8,128)} %copy-done.2, pred[]{:T(512)S(6)} %eq.52, f32[1,256,2048]{1,2,0:T(8,128)} %get-tuple-element.96, f32[]{:T(128)} %bitcast.3), kind=kLoop, calls=%fused_computation.18 | loop fusion | flops 2097152 | bytes 8388613 | tf_op jit(solution)/shard_map/add | solution.py:170
  369.4 2.9 copy.45
  (26 shorter events, 0.2 us)
Async XLA Ops:
  7.2 2.7 copy-start
  7.2 3.9 %copy-start.5 = (bf16[2048,256]{1,0:T(8,128)(2,1)S(1)}, bf16[2048,256]{1,0:T(8,128)(2,1)}, u32[]{:S(2)}) copy-start(bf16[2048,256]{1,0:T(8,128)(2,1)} %param.14) | copy-start | bytes 3145732
  7.2 159.4 %all-gather.3.cloned.1.call-start = ((), (), s32[]{:S(2)}) async-start(), calls=%async_computation.2 | async-start | bytes 26738688 | tf_op jit(solution)/shard_map/all_gather | solution.py:154
  11.3 4.9 %copy-start.4 = (f32[1,256,2048]{2,1,0:T(8,128)S(1)}, f32[1,256,2048]{2,1,0:T(8,128)}, u32[]{:S(2)}) copy-start(f32[1,256,2048]{2,1,0:T(8,128)} %param.12) | copy-start | bytes 6291460
  183.3 51.7 %all-to-all-start = ((bf16[256,16,1,384]{3,0,2,1:T(8,128)(2,1)}), bf16[256,16,1,384]{3,0,2,1:T(8,128)(2,1)}, u32[]{:S(2)}, u32[]{:S(2)}) async-start(bf16[256,16,1,384]{3,0,2,1:T(8,128)(2,1)} %maximum_bitcast_fusion), calls=%async_computation | async-start | bytes 6291456 | tf_op jit(solution)/shard_map/all_to_all | solution.py:159
  268.7 19.1 %all-to-all-start.1 = ((bf16[16,2,16384]{2,1,0:T(2,128)(2,1)}), bf16[16,2,16384]{2,1,0:T(2,128)(2,1)S(1)}, u32[]{:S(2)}, u32[]{:S(2)}) async-start(bf16[16,2,16384]{2,1,0:T(2,128)(2,1)} %reshape.238), calls=%async_computation.1 | async-start | bytes 2097152 | tf_op jit(solution)/shard_map/all_to_all | solution.py:161
  272.9 77.9 %all-gather.5.cloned.1.call-start = ((), (), s32[]{:S(2)}) async-start(), calls=%async_computation.3 | async-start | bytes 9437184 | tf_op jit(solution)/shard_map/all_gather | solution.py:11
  275.0 22.4 %copy-start.2 = (f32[1,256,2048]{1,2,0:T(8,128)}, f32[1,256,2048]{1,2,0:T(8,128)S(1)}, u32[]{:S(2)}) copy-start(f32[1,256,2048]{1,2,0:T(8,128)S(1)} %copy.42) | copy-start | bytes 6291460
  300.7 2.0 copy-start.3
  365.3 7.0 %copy-start.1 = (bf16[512,2048]{1,0:T(8,128)(2,1)S(1)}, bf16[512,2048]{1,0:T(8,128)(2,1)}, u32[]{:S(2)}) copy-start(bf16[512,2048]{1,0:T(8,128)(2,1)} %param.16) | copy-start | bytes 6291460
Sparse Core Ops, SparseCore 0:
  10.2 156.4 all-gather.2
  302.2 48.5 all-gather.4
where the time goes:
time: 380 us; the launch traced here: 379 us
  waiting for transfers between devices  252 us (66%)
  matrix products  43.1 us (11%)
  other arithmetic  30.8 us (8%)
  local copies, waits for them, and re-layouts  28.1 us (7%)
  between operations  15.5 us (4%)
  starting transfers between devices  9.42 us (2%)
    all_gather x1, waiting for transfers between devices, on_device(): lax.all_gather(query_key_value_weight, 'seq', axis=1, tiled=True)  147 us
    all_to_all x1, waiting for transfers between devices, on_device(): lax.all_to_all(grouped, 'seq', split_axis=1, concat_axis=0, tiled=True)  46.7 us
    all_gather x1, waiting for transfers between devices, entering(): gathered = lax.all_gather(x.astype(jnp.bfloat16), axis)  46.4 us
    unnamed x18, local copies, waits for them, and re-layouts  16.5 us
    dot_general x8, matrix products, one_block(): jnp.dot(weights.astype(jnp.bfloat16), values, preferred_element_type=jnp....  15.9 us
    add x7, other arithmetic, add_terms(): return earlier + later  12.2 us
    dot_general x1, matrix products, on_device(): jnp.einsum('td,dhe->the', normed, lax.all_gather(query_key_value_weight,...  11.6 us
    dot_general x8, matrix products, one_block(): jnp.einsum('qd,kd->qk', query_rows, keys, preferred_element_type=jnp.floa...  11.4 us
  transfers between devices with their start and end apart: 4, of which 4 were waited for; matrix products, arithmetic and copies ran while one was open for 4% of the time, Pallas kernels for 0%

commit v1 on v0

v1 whole, which is shorter than its diff:
```python
import functools
import math

import jax
import jax.numpy as jnp
from jax import lax
from jax.experimental import pallas as pl
from jax.experimental.pallas import tpu as pltpu
from jax.sharding import PartitionSpec as P

MESH = pl.DeviceIdType.MESH
F32, BF16 = jnp.float32, jnp.bfloat16


def place():
    step, seq = lax.axis_index("step"), lax.axis_index("seq")
    return step // 2, step % 2, seq // 4, seq % 4


def at(dy=0, dc=0, dz=0, dx=0):
    y, c, z, x = place()
    return (
        lax.rem(y + dy + 4, 4) * 2 + lax.rem(c + dc, 2),
        lax.rem(z + dz + 4, 4) * 4 + lax.rem(x + dx + 4, 4),
    )


def remote(src, dst, send, recv, device):
    return pltpu.make_async_remote_copy(
        src_ref=src, dst_ref=dst, send_sem=send, recv_sem=recv, device_id=device, device_id_type=MESH
    )


PARTNERS = (
    dict(dx=1), dict(dx=-1), dict(dz=1), dict(dz=-1), dict(dz=2),
    dict(dy=1), dict(dy=-1), dict(dy=2), dict(dc=1),
)


def project_kernel(
    x_ref, shift_ref, scale_ref, w_ref, out_ref,
    wbuf, xbuf, xm, stage, wl, w1s, w1r, w2s, w2r, wcs, wcr, xs, xr, fs, fr, qs, qr,
):
    y, c, z, x = place()
    barrier = pltpu.get_barrier_semaphore()
    for partner in PARTNERS:
        pl.semaphore_signal(barrier, inc=1, device_id=at(**partner), device_id_type=MESH)
    pl.semaphore_wait(barrier, len(PARTNERS))

    eighth = pl.ds(pl.multiple_of((c * 4 + y) * 256, 256), 256)
    half = pl.ds(pl.multiple_of(c * 1024, 1024), 1024)
    waits = []

    first = {}
    for j in (1, 3, 2):
        first[j] = remote(w_ref.at[eighth], wbuf.at[j, eighth], w1s.at[j], w1r.at[j], at(dz=-j))
        first[j].start()
        waits.append(first[j])
    own = pltpu.make_async_copy(w_ref, wbuf.at[0], wl)
    own.start()

    value = x_ref[...]
    spread = lax.rsqrt(jnp.mean(value * value, axis=-1, keepdims=True) + 1e-6)
    xbuf[0] = (value * spread).astype(BF16)
    top, bottom = pl.ds(0, 128), pl.ds(128, 128)
    toward = {}
    for part, rows in ((0, top), (1, bottom)):
        toward[3, part] = remote(xbuf.at[0, rows], xbuf.at[3, rows], xs.at[3, part], xr.at[3, part], at(dx=1))
    for part, rows in ((1, bottom), (0, top)):
        toward[1, part] = remote(xbuf.at[0, rows], xbuf.at[1, rows], xs.at[1, part], xr.at[1, part], at(dx=-1))
    for key in ((3, 0), (1, 1), (3, 1), (1, 0)):
        toward[key].start()
        waits.append(toward[key])

    def modulate(slot):
        xm[...] = (xbuf[slot].astype(F32) * (1.0 + scale_ref[...]) + shift_ref[...]).astype(BF16)

    second, sibling = {}, {}

    def spread_w(j):
        first[j].wait_recv()
        for i, dy in enumerate((1, -1, 2)):
            second[j, i] = remote(wbuf.at[j, eighth], wbuf.at[j, eighth], w2s.at[j, i], w2r.at[j, i], at(dy=dy))
            second[j, i].start()
            waits.append(second[j, i])

    def share_w(j):
        for i in range(3):
            second[j, i].wait_recv()
        sibling[j] = remote(wbuf.at[j, half], wbuf.at[j, half], wcs.at[j], wcr.at[j], at(dc=1))
        sibling[j].start()
        waits.append(sibling[j])

    factor = 2.5 / math.sqrt(128) * math.log2(math.e)
    outgoing = []

    def unit(block, j):
        p = jnp.dot(xm[...], wbuf[j], preferred_element_type=F32)
        q, k, v = p[:, :128], p[:, 128:256], p[:, 256:]
        q = q * (lax.rsqrt(jnp.mean(q * q, axis=-1, keepdims=True) + 1e-6) * factor)
        k = k * lax.rsqrt(jnp.mean(k * k, axis=-1, keepdims=True) + 1e-6)
        rows = pl.ds(pl.multiple_of((z * 4 + lax.rem(x + block, 4)) * 256, 256), 256)
        if j == 0:
            target = out_ref.at[rows]
        else:
            target = stage.at[j - 1, block]
        target[:, :128] = q.astype(BF16)
        target[:, 128:256] = k.astype(BF16)
        target[:, 256:] = v.astype(BF16)
        if j:
            copy = remote(stage.at[j - 1, block], out_ref.at[rows], qs.at[j - 1, block], qr.at[j - 1, block], at(dz=j))
            copy.start()
            outgoing.append(copy)

    modulate(0)
    spread_w(1)
    spread_w(3)
    spread_w(2)
    own.wait()
    unit(0, 0)
    toward[3, 0].wait_recv()
    fwd3 = remote(xbuf.at[3, top], xbuf.at[2, top], fs.at[0], fr.at[0], at(dx=1))
    fwd3.start()
    toward[1, 1].wait_recv()
    fwd1 = remote(xbuf.at[1, bottom], xbuf.at[2, bottom], fs.at[1], fr.at[1], at(dx=-1))
    fwd1.start()
    share_w(1)
    share_w(3)
    sibling[1].wait_recv()
    unit(0, 1)
    sibling[3].wait_recv()
    unit(0, 3)
    share_w(2)
    sibling[2].wait_recv()
    unit(0, 2)
    toward[3, 1].wait_recv()
    modulate(3)
    for j in (1, 3, 2, 0):
        unit(3, j)
    toward[1, 0].wait_recv()
    modulate(1)
    for j in (1, 3, 2, 0):
        unit(1, j)
    fwd3.wait_recv()
    fwd1.wait_recv()
    modulate(2)
    for j in (1, 3, 2, 0):
        unit(2, j)
    fwd3.wait_send()
    fwd1.wait_send()
    for copy in waits:
        copy.wait_send()
    for copy in outgoing:
        copy.wait()


def project(x, shift, scale, w):
    vm = pl.BlockSpec(memory_space=pltpu.VMEM)
    dma = pltpu.SemaphoreType.DMA
    return pl.pallas_call(
        project_kernel,
        out_shape=jax.ShapeDtypeStruct((4096, 384), BF16),
        in_specs=[vm, vm, vm, pl.BlockSpec(memory_space=pl.ANY)],
        out_specs=vm,
        scratch_shapes=[
            pltpu.VMEM((4, 2048, 384), BF16),
            pltpu.VMEM((4, 256, 2048), BF16),
            pltpu.VMEM((256, 2048), BF16),
            pltpu.VMEM((3, 4, 256, 384), BF16),
            dma, dma((4,)), dma((4,)), dma((4, 3)), dma((4, 3)), dma((4,)), dma((4,)),
            dma((4, 2)), dma((4, 2)), dma((2,)), dma((2,)), dma((3, 4)), dma((3, 4)),
        ],
        compiler_params=pltpu.CompilerParams(
            collective_id=1, has_side_effects=True, vmem_limit_bytes=56 * 1024 * 1024
        ),
    )(x, shift, scale, w)


def attend_kernel(pieces, kb, qkv, gd_ref, x_ref, mixed, pin, v1, ostage, pout, os, orr, ls, cs, cr):
    step, seq = lax.axis_index("step"), lax.axis_index("seq")
    R = 256 // pieces
    barrier = pltpu.get_barrier_semaphore()

    def peer(o):
        return (step, lax.rem(seq + o, 16))

    after = (lax.rem(step + 1, 8), seq)
    before = (lax.rem(step + 7, 8), seq)
    for o in range(1, 16):
        pl.semaphore_signal(barrier, inc=1, device_id=peer(o), device_id_type=MESH)
    for d in (after, before):
        pl.semaphore_signal(barrier, inc=1, device_id=d, device_id_type=MESH)
    v1[:, :128] = qkv[:, 256:]
    v1[:, 128:] = jnp.ones((4096, 128), BF16)
    pl.semaphore_wait(barrier, 17)
    mine = pl.ds(pl.multiple_of(seq * 128, 128), 128)

    def rows_of(p):
        return pl.ds(pl.multiple_of(p * R, R), R)

    def out_copy(p, o):
        to = lax.rem(seq + o, 16)
        return remote(ostage.at[p, to], mixed.at[rows_of(p), mine], os.at[p, o - 1], orr.at[p, o - 1], peer(o))

    def local_copy(p):
        return pltpu.make_async_copy(ostage.at[p, seq], mixed.at[rows_of(p), mine], ls.at[p])

    def chain_copy(p):
        return remote(pout.at[rows_of(p)], pin.at[rows_of(p)], cs.at[p], cr.at[p], after)

    def attend(p):
        q = jnp.concatenate([qkv[pl.ds(pl.multiple_of(s * 256 + p * R, R), R), :128] for s in range(16)], axis=0)
        acc = jnp.zeros((16 * R, 256), F32)
        for j in range(4096 // kb):
            s = lax.dot_general(q, qkv[j * kb:(j + 1) * kb, 128:256], (((1,), (1,)), ((), ())), preferred_element_type=F32)
            acc += jnp.dot(jnp.exp2(s).astype(BF16), v1[j * kb:(j + 1) * kb], preferred_element_type=F32)
        o = (acc[:, :128] / acc[:, 128:]).astype(BF16)
        for s in range(16):
            ostage[p, s] = o[s * R:(s + 1) * R]
        local_copy(p).start()
        for o in range(1, 16):
            out_copy(p, o).start()

    def chain(p):
        rows = rows_of(p)
        for o in range(1, 16):
            out_copy(p, o).wait_recv()
        local_copy(p).wait()

        @pl.when(step == 0)
        def _():
            pout[rows] = (x_ref[rows] + gd_ref[...] * mixed[rows].astype(F32)).astype(BF16)

        @pl.when(step > 0)
        def _():
            chain_copy(p).wait_recv()
            pout[rows] = (pin[rows].astype(F32) + gd_ref[...] * mixed[rows].astype(F32)).astype(BF16)

        @pl.when(step < 7)
        def _():
            chain_copy(p).start()

    def body(p, carry):
        attend(p)

        @pl.when(p > 0)
        def _():
            chain(p - 1)
        return carry

    lax.fori_loop(0, pieces, body, 0)
    chain(pieces - 1)

    @pl.when(step == 0)
    def _():
        pin[...] = jnp.zeros_like(pin)

    def drain(p, carry):
        for o in range(1, 16):
            out_copy(p, o).wait_send()

        @pl.when(step < 7)
        def _():
            chain_copy(p).wait_send()
        return carry

    lax.fori_loop(0, pieces, drain, 0)


def attend(qkv, gd, x, pieces=8, kb=4096):
    vm = pl.BlockSpec(memory_space=pltpu.VMEM)
    dma = pltpu.SemaphoreType.DMA
    R = 256 // pieces
    return pl.pallas_call(
        functools.partial(attend_kernel, pieces, kb),
        out_shape=(jax.ShapeDtypeStruct((256, 2048), BF16), jax.ShapeDtypeStruct((256, 2048), BF16)),
        in_specs=[vm, vm, vm],
        out_specs=(vm, vm),
        scratch_shapes=[
            pltpu.VMEM((4096, 256), BF16),
            pltpu.VMEM((pieces, 16, R, 128), BF16),
            pltpu.VMEM((256, 2048), BF16),
            dma((pieces, 15)), dma((pieces, 15)), dma((pieces,)), dma((pieces,)), dma((pieces,)),
        ],
        compiler_params=pltpu.CompilerParams(
            collective_id=2, has_side_effects=True, vmem_limit_bytes=56 * 1024 * 1024
        ),
    )(qkv, gd, x)


def embed_time(timestep_markers, hidden_width):
    half = hidden_width // 2
    freqs = jnp.exp(-math.log(10000.0) * jnp.arange(half, dtype=jnp.float32) / half)
    angles = timestep_markers[:, None] * freqs[None, :]
    return jnp.concatenate([jnp.cos(angles), jnp.sin(angles)], axis=1)


def apply_modulation(
    timestep_markers,
    action_embedding_matrix,
    action_token_index,
    modulation_down_weight,
    modulation_up_weight,
):
    hidden_width = action_embedding_matrix.shape[1]
    onehot = (
        action_token_index[:, None]
        == jnp.arange(action_embedding_matrix.shape[0], dtype=jnp.int32)[None, :]
    ).astype(jnp.bfloat16)
    action_mean = jnp.mean(
        jnp.dot(onehot, action_embedding_matrix, preferred_element_type=jnp.float32), axis=0
    )
    conditioning_vector = jax.nn.silu(
        embed_time(timestep_markers, hidden_width) + action_mean[None, :]
    ).astype(jnp.bfloat16)
    reduced_rank_update = jnp.dot(
        conditioning_vector, modulation_down_weight, preferred_element_type=jnp.float32
    ).astype(jnp.bfloat16)
    return jnp.dot(
        reduced_rank_update, modulation_up_weight, preferred_element_type=jnp.float32
    ).reshape(timestep_markers.shape[0], 3, hidden_width)


def on_device(
    iterate,
    query_key_value_weight,
    modulation_down_weight,
    modulation_up_weight,
    action_embedding_matrix,
    action_token_index,
    sched,
    window,
):
    step_count = iterate.shape[0]
    first_step = lax.axis_index("step") * step_count
    position = first_step + jnp.arange(step_count + 1, dtype=jnp.int32)
    chosen = jnp.sum(
        jnp.where(
            position[:, None] == jnp.arange(window.shape[0], dtype=jnp.int32)[None, :],
            window[None, :],
            0,
        ),
        axis=1,
    )
    stamps_int = jnp.sum(
        jnp.where(
            chosen[:, None] == jnp.arange(sched.shape[0], dtype=jnp.int32)[None, :],
            sched[None, :],
            0,
        ),
        axis=1,
    )
    timestep_markers = stamps_int.astype(jnp.float32)
    sigma = timestep_markers / 1000.0
    delta = sigma[1:] - sigma[:-1]
    modulation_factors = apply_modulation(
        timestep_markers[:-1],
        action_embedding_matrix,
        action_token_index,
        modulation_down_weight,
        modulation_up_weight,
    )
    shift, scale, gate = (modulation_factors[:, i] for i in range(3))
    rows = iterate[0]
    packed = project(rows, shift, scale, query_key_value_weight[:, 0])
    mixed, earlier = attend(packed, delta[:, None] * gate, rows)
    velocity = gate * mixed.astype(F32)
    entering = jnp.where(first_step == 0, rows, earlier.astype(F32))
    new_states = entering + delta[:, None] * velocity
    return (new_states[None], velocity[None])


def solution(mesh):
    placed = (P("step", "seq", None), P(None, "seq", None), P(), P(), P(), P(), P(), P())
    return jax.shard_map(
        on_device,
        mesh=mesh,
        in_specs=placed,
        out_specs=(P("step", "seq", None), P("step", "seq", None)),
        check_vma=False,
    )
```

time: 380 us -> 152 us (0.40)
  waiting for transfers between devices: 252 us -> 0 us
  Pallas kernels: 0 us -> 133 us
  matrix products: 43.1 us -> 4.13 us
  other arithmetic: 30.8 us -> 6.83 us
  local copies, waits for them, and re-layouts: 28.1 us -> 5.87 us
  between operations: 15.5 us -> 2.05 us
  starting transfers between devices: 9.42 us -> 0 us
    all_gather x2 -> x0, waiting for transfers between devices: 194 us -> none  [the longest x1 147 us: on_device(): lax.all_gather(query_key_value_weight, 'seq', axis=1, tiled=True)]
    pallas_call x0 -> x2, Pallas kernels: none -> 133 us  [the longest x1 75.4 us: project(): pl.pallas_call(project_kernel, out_shape=jax.ShapeDtypeStruct((4096, 384)...]
    all_to_all x2 -> x0, waiting for transfers between devices: 57.5 us -> none  [the longest x1 46.7 us: on_device(): lax.all_to_all(grouped, 'seq', split_axis=1, concat_axis=0, tiled=True)]
    dot_general x17 -> x0, matrix products: 39 us -> none  [the longest x8 15.9 us: one_block(): jnp.dot(weights.astype(jnp.bfloat16), values, preferred_element_type=jnp....]
    add x9 -> x0, other arithmetic: 16.3 us -> none  [the longest x7 12.2 us: add_terms(): return earlier + later]
    unnamed x18 -> x7, local copies, waits for them, and re-layouts: 16.5 us -> 4.67 us
    all_to_all x2 -> x0, starting transfers between devices: 9.15 us -> none  [the longest x1 5.05 us: on_device(): lax.all_to_all(grouped, 'seq', split_axis=1, concat_axis=0, tiled=True)]
    convert_element_type x2 -> x0, other arithmetic: 4.79 us -> none  [the longest x1 3.26 us: entering(): gathered = lax.all_gather(x.astype(jnp.bfloat16), axis)]
  transfers between devices with their start and end apart: 4 -> 0, of which waited for: 4 -> 0; matrix products, arithmetic and copies ran while one was open for 4% -> 0% of each run, Pallas kernels for 0% -> 0%
where the time goes in v1:
time: 152 us
  Pallas kernels  133 us (88%)
  other arithmetic  6.83 us (4%)
  local copies, waits for them, and re-layouts  5.87 us (4%)
  matrix products  4.13 us (3%)
  between operations  2.05 us (1%)
    pallas_call x1, Pallas kernels, project(): pl.pallas_call(project_kernel, out_shape=jax.ShapeDtypeStruct((4096, 384)...  75.4 us
    pallas_call x1, Pallas kernels, attend(): pl.pallas_call(functools.partial(attend_kernel, pieces, kb), out_shape=(j...  57.3 us
    unnamed x7, local copies, waits for them, and re-layouts  4.67 us
    broadcast_in_dim x1, other arithmetic, on_device(): return (new_states[None], velocity[None])  4.27 us

profile of v1, /device:TPU:25, one launch (start us, length us, event | category | flops | bytes accessed | tf_op | source)
XLA Modules:
  0.0 151.6 jit_solution(2343551698901099878)
XLA Ops:
  0.6 0.0 copy-start
  0.6 0.0 copy-start.2
  0.7 1.0 fusion.5
  1.7 0.8 fusion.6
  2.5 0.6 fusion.8
  4.4 0.1 fusion.3
  4.5 0.0 copy-done
  4.5 1.1 convolution_reduce_fusion
  5.6 0.0 copy-done.2
  5.6 0.2 fusion.9
  5.9 4.6 %copy.11 = bf16[256,6144]{0,1:T(8,128)(2,1)} copy(bf16[256,6144]{1,0:T(8,128)(2,1)} %param.11) | data formatting | bytes 6291456 | tf_op args[3]
  10.5 2.8 %fusion.10 = f32[1,3,2048]{2,0,1:T(1,128)S(1)} fusion(bf16[256,1,1]{0,1,2:T(2,128)(2,1)S(1)} %reshape.72, bf16[3,2048,256]{2,1,0:T(8,128)(2,1)} %bitcast.38), kind=kOutput, calls=%fused_computation.24 | convolution fusion | flops 3145728 | bytes 3170816 | tf_op jit(solution)/shard_map/dot_general | solution.py:319
  13.3 0.6 fusion.2.gd_ref
  14.0 0.6 fusion.7
  14.6 75.4 %shard_map.95.qkv = bf16[4096,384]{1,0:T(8,128)(2,1)} custom-call(f32[256,2048]{1,0:T(8,128)} %bitcast.36, f32[1,2048]{1,0:T(1,128)} %get-tuple-element.10.shift_ref, f32[1,2048]{1,0:T(1,128)} %get-tuple-element.9.scale_ref, bf16[2048,384]{1,0:T(8,128)(2,1)} %bitcast.39), custom_call_target="tpu_custom_call" | custom-call | tf_op jit(solution)/shard_map/pallas_call | solution.py:160
  90.0 0.0 copy-start.1
  90.0 57.3 %shard_map.96 = (bf16[256,2048]{1,0:T(8,128)(2,1)}, bf16[256,2048]{1,0:T(8,128)(2,1)}) custom-call(bf16[4096,384]{1,0:T(8,128)(2,1)} %shard_map.95.qkv, f32[1,2048]{1,0:T(1,128)} %fusion.2.gd_ref, f32[256,2048]{1,0:T(8,128)} %bitcast.37), custom_call_target="tpu_custom_call" | custom-call | tf_op jit(solution)/shard_map/pallas_call | solution.py:274
  147.3 0.0 copy-done.1
  147.3 4.3 %fusion = (f32[1,256,2048]{2,1,0:T(8,128)}, f32[1,256,2048]{2,1,0:T(8,128)}) fusion(bf16[256,2048]{1,0:T(8,128)(2,1)} %get-tuple-element.5, f32[2048]{0:T(1024)S(1)} %bitcast.40, f32[]{:T(128)} %bitcast.9, bf16[256,2048]{1,0:T(8,128)(2,1)} %get-tuple-element.4, f32[1,256,2048]{2,1,0:T(8,128)S(1)} %copy-done.1, pred[]{:T(512)S(6)} %eq.20), kind=kLoop, calls=%fused_computation.2 | loop fusion | flops 3145728 | bytes 8396805 | tf_op jit(solution)/shard_map/broadcast_in_dim | solution.py:370
  (7 shorter events, 0.0 us)
Async XLA Ops:
  0.6 3.9 %copy-start = (bf16[512,2048]{1,0:T(8,128)(2,1)S(1)}, bf16[512,2048]{1,0:T(8,128)(2,1)}, u32[]{:S(2)}) copy-start(bf16[512,2048]{1,0:T(8,128)(2,1)} %param.12) | copy-start | bytes 6291460
  0.6 5.0 %copy-start.2 = (bf16[2048,256]{1,0:T(8,128)(2,1)S(1)}, bf16[2048,256]{1,0:T(8,128)(2,1)}, u32[]{:S(2)}) copy-start(bf16[2048,256]{1,0:T(8,128)(2,1)} %param.10) | copy-start | bytes 3145732
  90.0 57.4 %copy-start.1 = (f32[1,256,2048]{2,1,0:T(8,128)S(1)}, f32[1,256,2048]{2,1,0:T(8,128)}, u32[]{:S(2)}) copy-start(f32[1,256,2048]{2,1,0:T(8,128)} %param.8) | copy-start | bytes 6291460

commit v2 on v0

v2 whole, which is shorter than its diff:
```python
import math

import jax
import jax.numpy as jnp
from jax import lax
from jax.experimental import pallas as pl
from jax.experimental.pallas import tpu as pltpu
from jax.sharding import PartitionSpec as P

MESH = pl.DeviceIdType.MESH
F32, BF16 = jnp.float32, jnp.bfloat16
PIECES = 8
PIECE = 256 // PIECES
KEYS = 2048
FACTOR = 2.5 / math.sqrt(128) * math.log2(math.e)


def remote(src, dst, send, recv, device):
    return pltpu.make_async_remote_copy(
        src_ref=src, dst_ref=dst, send_sem=send, recv_sem=recv, device_id=device, device_id_type=MESH
    )


def inverse_rms(value):
    return lax.rsqrt(jnp.mean(value * value, axis=-1, keepdims=True) + 1e-6)


def sweep_kernel(
    ids, sched, window, x_ref, w_ref, ae_ref, md_ref, mu_ref,
    mixed, pin, gate_ref, delta_ref,
    xbuf, wraw, wmod, bias, ae, md, mu, qkv, v1, ostage, pout, gd,
    load_sem, home_s, home_r, guest_s, guest_r, share_s, share_r, wx_s, wx_r,
    hop_s, hop_r, out_s, out_r, chain_s, chain_r,
):
    step, seq = lax.axis_index("step"), lax.axis_index("seq")
    y, c = step // 2, lax.rem(step, 2)
    z, x = seq // 4, lax.rem(seq, 4)
    m = x // 2
    stays = c == m
    head = jnp.where(c == 0, seq, z * 4 + 3 - x)

    def device(core, dz, column):
        return (y * 2 + core, lax.rem(z + dz + 4, 4) * 4 + column)

    mate = device(c, 0, x + 1 - 2 * lax.rem(x, 2))
    up, down = device(c, 1, x), device(c, -1, x)
    sibling = device(1 - c, 0, x)
    across = [device(core, 0, 3 - x) for core in range(2)]
    after = (lax.rem(step + 1, 8), seq)
    before = (lax.rem(step + 7, 8), seq)

    barrier = pltpu.get_barrier_semaphore()
    for other in (mate, up, down, sibling, *across, after, before):
        pl.semaphore_signal(barrier, inc=1, device_id=other, device_id_type=MESH)
    for other_z in range(4):
        for column in range(2):
            for core in range(2):
                source = (y * 2 + core, other_z * 4 + 2 * c + column)
                itself = jnp.logical_and(core == c, other_z * 4 + 2 * c + column == seq)

                @pl.when(jnp.logical_not(itself))
                def _():
                    pl.semaphore_signal(barrier, inc=1, device_id=source, device_id_type=MESH)

    loads = [
        pltpu.make_async_copy(ae_ref, ae, load_sem.at[0]),
        pltpu.make_async_copy(md_ref, md, load_sem.at[1]),
        pltpu.make_async_copy(mu_ref, mu, load_sem.at[2]),
    ]
    for load in loads:
        load.start()
    own_w = pltpu.make_async_copy(w_ref, wraw, load_sem.at[3])

    @pl.when(c == 0)
    def _():
        own_w.start()

    mine = pl.ds(pl.multiple_of(c * 128, 128), 128)
    theirs = pl.ds(pl.multiple_of((1 - c) * 128, 128), 128)

    value = x_ref[...]
    unit = (value * inverse_rms(value)).astype(BF16)

    home_out = [
        remote(xbuf.at[0, theirs], xbuf.at[0, theirs], home_s.at[0], home_r.at[0], sibling),
        remote(xbuf.at[0, mine], xbuf.at[0, mine], home_s.at[1], home_r.at[1], sibling),
    ]
    guest_out = [
        remote(pout.at[pl.ds(core * 128, 128)], xbuf.at[1, pl.ds(core * 128, 128)], guest_s.at[core], guest_r, across[core])
        for core in range(2)
    ]

    pl.semaphore_wait(barrier, 8 + 16 - stays.astype(jnp.int32))

    @pl.when(stays)
    def _():
        xbuf[0] = unit
        home_out[0].start()

    @pl.when(jnp.logical_not(stays))
    def _():
        pout[...] = unit
        for copy in guest_out:
            copy.start()
        home_out[0].wait_recv()

    hops = []

    def hop(index, slot, to, to_slot, first=0, count=128):
        rows = pl.ds(pl.multiple_of(c * 128 + first, 32), count)
        copy = remote(xbuf.at[slot, rows], xbuf.at[to_slot, rows], hop_s.at[index], hop_r.at[index], to)
        hops.append(copy)
        return copy

    shares = {}

    def share(slot):
        shares[slot] = remote(xbuf.at[slot, mine], xbuf.at[slot, mine], share_s.at[slot], share_r.at[slot], sibling)
        shares[slot].start()

    h01 = hop(0, 0, mate, 2)
    h30 = hop(1, 0, up, 12)
    h10 = hop(2, 0, down, 4)
    for copy in (h01, h30, h10):
        copy.start()

    @pl.when(stays)
    def _():
        home_out[1].start()

    stamps = [sched[window[2 * y + i]].astype(F32) for i in range(3)]
    row8 = lax.broadcasted_iota(jnp.int32, (8, 1024), 0)
    lane = lax.broadcasted_iota(jnp.int32, (8, 1024), 1).astype(F32)
    angles = jnp.where(row8 == 0, stamps[0], stamps[1]) * jnp.exp(-math.log(10000.0) / 1024 * lane)
    temb = jnp.concatenate([jnp.cos(angles), jnp.sin(angles)], axis=1)
    vocab = lax.broadcasted_iota(jnp.int32, (16, 512), 1)
    counts = jnp.zeros((16, 512), F32)
    for i in range(12):
        counts += (vocab == ids[i]).astype(F32)
    for load in loads:
        load.wait()
    mean = jnp.dot(counts.astype(BF16), ae[...], preferred_element_type=F32)[:8] / 12.0
    cond = temb + mean
    cond = (cond / (1.0 + jnp.exp(-cond))).astype(BF16)
    low = jnp.dot(cond, md[...], preferred_element_type=F32).astype(BF16)
    factors = jnp.dot(low, mu[...], preferred_element_type=F32)
    scale_cols = lax.dot_general(
        mu[:, 2048:4096], low, (((0,), (1,)), ((), ())), preferred_element_type=F32
    )
    rows = lax.broadcasted_iota(jnp.int32, (8, 2048), 0)
    gate = jnp.sum(jnp.where(rows == c, factors[:, 4096:], 0.0), axis=0, keepdims=True)
    delta = jnp.where(c == 0, stamps[1] / 1000.0 - stamps[0] / 1000.0, stamps[2] / 1000.0 - stamps[1] / 1000.0)
    gate_ref[...] = gate
    delta_ref[...] = jnp.full((1, 128), delta, F32)
    gd[...] = gate * delta
    columns = lax.broadcasted_iota(jnp.int32, (2048, 8), 1)
    scale = jnp.sum(jnp.where(columns == m, scale_cols, 0.0), axis=1, keepdims=True)
    shift = factors[:, :2048]
    shift_high = shift.astype(BF16)
    shift_low = (shift - shift_high.astype(F32)).astype(BF16)

    guest_out[0].wait_recv()
    g01, g30, g10 = hop(3, 1, mate, 3), hop(4, 1, up, 13), hop(5, 1, down, 5)
    for copy in (g01, g30, g10):
        copy.start()
    w_across = remote(w_ref, wraw, wx_s, wx_r, across[1])

    @pl.when(c == 1)
    def _():
        w_across.start()

    share(1)
    h30.wait_recv()
    h20, x31h = hop(6, 12, up, 8), hop(7, 12, mate, 14)
    h20.start()
    x31h.start()
    share(12)
    h10.wait_recv()
    x11h = hop(8, 4, mate, 6)
    x11h.start()
    share(4)
    h01.wait_recv()
    share(2)

    g01.wait_recv()
    g31, g11 = hop(9, 3, up, 15), hop(10, 3, down, 7)
    g31.start()
    g11.start()
    share(3)
    g10.wait_recv()
    g20 = hop(11, 5, down, 9)
    g20.start()
    share(5)
    g30.wait_recv()
    share(13)

    @pl.when(c == 0)
    def _():
        own_w.wait()

    @pl.when(c == 1)
    def _():
        w_across.wait_recv()

    for i in range(4):
        part = pl.ds(i * 512, 512)
        wmod[part] = (wraw[part].astype(F32) * (1.0 + scale[i * 512:(i + 1) * 512])).astype(BF16)
    shifted = jnp.dot(shift_high, wraw[...], preferred_element_type=F32)
    shifted += jnp.dot(shift_low, wraw[...], preferred_element_type=F32)
    rows = lax.broadcasted_iota(jnp.int32, (8, 384), 0)
    bias[...] = jnp.sum(jnp.where(rows == m, shifted, 0.0), axis=0, keepdims=True)
    v1[:, 128:] = jnp.ones((4096, 128), BF16)

    def project(slot):
        zr, kind = slot // 4, slot % 4
        other = x + 1 - 2 * lax.rem(x, 2)
        column = (x, 3 - x, other, 3 - other)[kind]
        block = lax.rem(z + zr, 4) * 4 + column
        p = jnp.dot(xbuf[slot], wmod[...], preferred_element_type=F32) + bias[...]
        q, k = p[:, :128], p[:, 128:256]
        rows = pl.ds(pl.multiple_of(block * 256, 256), 256)
        qkv[rows, :128] = (q * (inverse_rms(q) * FACTOR)).astype(BF16)
        qkv[rows, 128:] = (k * inverse_rms(k)).astype(BF16)
        v1[rows, :128] = p[:, 256:].astype(BF16)

    @pl.when(jnp.logical_not(stays))
    def _():
        home_out[1].wait_recv()

    project(0)
    for slot in (1, 12, 4, 2):
        shares[slot].wait_recv()
        project(slot)

    x11h.wait_recv()
    part11 = hop(12, 6, down, 10, 32, 32)
    part11.start()
    share(6)
    h20.wait_recv()
    part20 = hop(13, 8, mate, 10, 64, 64)
    part20.start()
    share(8)
    g20.wait_recv()
    share(9)
    for slot in (3, 5, 13):
        shares[slot].wait_recv()
        project(slot)
    x31h.wait_recv()
    part31 = hop(14, 14, up, 10, 0, 32)
    part31.start()
    share(14)
    g31.wait_recv()
    part31g = hop(15, 15, up, 11, 0, 64)
    part31g.start()
    share(15)
    g11.wait_recv()
    part11g = hop(16, 7, down, 11, 64, 64)
    part11g.start()
    share(7)
    for slot in (6, 8, 9):
        shares[slot].wait_recv()
        project(slot)
    for slot in (14, 15, 7):
        shares[slot].wait_recv()
        project(slot)
    part31.wait_recv()
    part11.wait_recv()
    part20.wait_recv()
    share(10)
    part31g.wait_recv()
    part11g.wait_recv()
    share(11)
    for slot in (10, 11):
        shares[slot].wait_recv()
        project(slot)
    for copy in hops:
        copy.wait_send()
    for slot in shares:
        shares[slot].wait_send()

    @pl.when(stays)
    def _():
        for copy in home_out:
            copy.wait_send()

    @pl.when(jnp.logical_not(stays))
    def _():
        for copy in guest_out:
            copy.wait_send()

    @pl.when(c == 1)
    def _():
        w_across.wait_send()

    own_columns = pl.ds(pl.multiple_of(head * 128, 128), 128)

    def rows_of(p):
        return pl.ds(pl.multiple_of(p * PIECE, PIECE), PIECE)

    def out_copy(p, o):
        to = lax.rem(seq + o, 16)
        return remote(
            ostage.at[p, to], mixed.at[rows_of(p), own_columns], out_s.at[p, o], out_r.at[p, head], (y * 2 + m, to)
        )

    def keep_copy(p):
        return pltpu.make_async_copy(ostage.at[p, seq], mixed.at[rows_of(p), own_columns], out_r.at[p, head])

    def arrival(p, other):
        columns = pl.ds(other * 128, 128)
        return pltpu.make_async_copy(ostage.at[p, 0], mixed.at[rows_of(p), columns], out_r.at[p, other])

    def chain_copy(p):
        return remote(pout.at[rows_of(p)], pin.at[rows_of(p)], chain_s.at[p], chain_r.at[p], after)

    def attend(p):
        q = jnp.concatenate(
            [qkv[pl.ds(pl.multiple_of(s * 256 + p * PIECE, PIECE), PIECE), :128] for s in range(16)], axis=0
        )
        acc = jnp.zeros((16 * PIECE, 256), F32)
        for j in range(0, 4096, KEYS):
            s = lax.dot_general(
                q, qkv[j:j + KEYS, 128:], (((1,), (1,)), ((), ())), preferred_element_type=F32
            )
            acc += jnp.dot(jnp.exp2(s).astype(BF16), v1[j:j + KEYS], preferred_element_type=F32)
        o = (acc[:, :128] / acc[:, 128:]).astype(BF16)
        for s in range(16):
            ostage[p, s] = o[s * PIECE:(s + 1) * PIECE]

        @pl.when(stays)
        def _():
            keep_copy(p).start()

        @pl.when(jnp.logical_not(stays))
        def _():
            out_copy(p, 0).start()

        for o in range(1, 16):
            out_copy(p, o).start()

    def chain(p):
        rows = rows_of(p)
        for other in range(16):
            arrival(p, other).wait()

        @pl.when(step == 0)
        def _():
            pout[rows] = (x_ref[rows] + gd[...] * mixed[rows].astype(F32)).astype(BF16)

        @pl.when(step > 0)
        def _():
            chain_copy(p).wait_recv()
            pout[rows] = (pin[rows].astype(F32) + gd[...] * mixed[rows].astype(F32)).astype(BF16)

        @pl.when(step < 7)
        def _():
            chain_copy(p).start()

    def body(p, carry):
        attend(p)

        @pl.when(p > 0)
        def _():
            chain(p - 1)
        return carry

    lax.fori_loop(0, PIECES, body, 0)
    chain(PIECES - 1)

    @pl.when(step == 0)
    def _():
        pin[...] = jnp.zeros_like(pin)

    def drain(p, carry):
        @pl.when(jnp.logical_not(stays))
        def _():
            out_copy(p, 0).wait_send()

        for o in range(1, 16):
            out_copy(p, o).wait_send()

        @pl.when(step < 7)
        def _():
            chain_copy(p).wait_send()
        return carry

    lax.fori_loop(0, PIECES, drain, 0)


def sweep(ids, sched, window, x, w, ae, md, mu):
    vm = pl.BlockSpec(memory_space=pltpu.VMEM)
    sm = pl.BlockSpec(memory_space=pltpu.SMEM)
    anywhere = pl.BlockSpec(memory_space=pl.ANY)
    dma = pltpu.SemaphoreType.DMA
    return pl.pallas_call(
        sweep_kernel,
        out_shape=(
            jax.ShapeDtypeStruct((256, 2048), BF16), jax.ShapeDtypeStruct((256, 2048), BF16),
            jax.ShapeDtypeStruct((1, 2048), F32), jax.ShapeDtypeStruct((1, 128), F32),
        ),
        in_specs=[sm, sm, sm, vm, anywhere, anywhere, anywhere, anywhere],
        out_specs=(vm, vm, vm, vm),
        scratch_shapes=[
            pltpu.VMEM((16, 256, 2048), BF16),
            pltpu.VMEM((2048, 384), BF16),
            pltpu.VMEM((2048, 384), BF16),
            pltpu.VMEM((1, 384), F32),
            pltpu.VMEM((512, 2048), BF16),
            pltpu.VMEM((2048, 256), BF16),
            pltpu.VMEM((256, 6144), BF16),
            pltpu.VMEM((4096, 256), BF16),
            pltpu.VMEM((4096, 256), BF16),
            pltpu.VMEM((PIECES, 16, PIECE, 128), BF16),
            pltpu.VMEM((256, 2048), BF16),
            pltpu.VMEM((1, 2048), F32),
            dma((4,)), dma((2,)), dma((2,)), dma((2,)), dma, dma((16,)), dma((16,)), dma, dma,
            dma((17,)), dma((17,)), dma((PIECES, 16)), dma((PIECES, 16)), dma((PIECES,)), dma((PIECES,)),
        ],
        compiler_params=pltpu.CompilerParams(
            collective_id=1, has_side_effects=True, vmem_limit_bytes=60 * 1024 * 1024
        ),
    )(ids, sched, window, x, w, ae, md, mu)


def on_device(
    iterate,
    query_key_value_weight,
    modulation_down_weight,
    modulation_up_weight,
    action_embedding_matrix,
    action_token_index,
    sched,
    window,
):
    rows = iterate[0]
    mixed, earlier, gate, delta = sweep(
        action_token_index,
        sched,
        window,
        rows,
        query_key_value_weight[:, 0],
        action_embedding_matrix,
        modulation_down_weight,
        modulation_up_weight,
    )
    velocity = gate * mixed.astype(F32)
    entering = jnp.where(lax.axis_index("step") == 0, rows, earlier.astype(F32))
    new_states = entering + delta[:, :1] * velocity
    return (new_states[None], velocity[None])


def solution(mesh):
    placed = (P("step", "seq", None), P(None, "seq", None), P(), P(), P(), P(), P(), P())
    return jax.shard_map(
        on_device,
        mesh=mesh,
        in_specs=placed,
        out_specs=(P("step", "seq", None), P("step", "seq", None)),
        check_vma=False,
    )
```

time: 380 us -> 133 us (0.35)
  waiting for transfers between devices: 252 us -> 0 us
  Pallas kernels: 0 us -> 128 us
  matrix products: 43.1 us -> 0 us
  local copies, waits for them, and re-layouts: 28.1 us -> 0.01 us
  other arithmetic: 30.8 us -> 4.79 us
  between operations: 15.5 us -> 0.66 us
  starting transfers between devices: 9.42 us -> 0 us
    all_gather x2 -> x0, waiting for transfers between devices: 194 us -> none  [the longest x1 147 us: on_device(): lax.all_gather(query_key_value_weight, 'seq', axis=1, tiled=True)]
    pallas_call x0 -> x1, Pallas kernels: none -> 128 us  [sweep(): pl.pallas_call(sweep_kernel, out_shape=(jax.ShapeDtypeStruct((256, 2048),...]
    all_to_all x2 -> x0, waiting for transfers between devices: 57.5 us -> none  [the longest x1 46.7 us: on_device(): lax.all_to_all(grouped, 'seq', split_axis=1, concat_axis=0, tiled=True)]
    dot_general x20 -> x0, matrix products: 43.1 us -> none  [the longest x8 15.9 us: one_block(): jnp.dot(weights.astype(jnp.bfloat16), values, preferred_element_type=jnp....]
    unnamed x18 -> x2, local copies, waits for them, and re-layouts: 16.5 us -> 0.01 us
    add x10 -> x0, other arithmetic: 16.3 us -> none  [the longest x7 12.2 us: add_terms(): return earlier + later]
    all_to_all x2 -> x0, starting transfers between devices: 9.15 us -> none  [the longest x1 5.05 us: on_device(): lax.all_to_all(grouped, 'seq', split_axis=1, concat_axis=0, tiled=True)]
    convert_element_type x5 -> x0, other arithmetic: 4.82 us -> none  [the longest x1 3.26 us: entering(): gathered = lax.all_gather(x.astype(jnp.bfloat16), axis)]
  transfers between devices with their start and end apart: 4 -> 0, of which waited for: 4 -> 0; matrix products, arithmetic and copies ran while one was open for 4% -> 0% of each run, Pallas kernels for 0% -> 0%
where the time goes in v2:
time: 133 us
  Pallas kernels  128 us (96%)
  other arithmetic  4.79 us (4%)
    pallas_call x1, Pallas kernels, sweep(): pl.pallas_call(sweep_kernel, out_shape=(jax.ShapeDtypeStruct((256, 2048),...  128 us
    broadcast_in_dim x1, other arithmetic, on_device(): return (new_states[None], velocity[None])  4.79 us

profile of v2, /device:TPU:25, one launch (start us, length us, event | category | flops | bytes accessed | tf_op | source)
XLA Modules:
  0.0 133.2 jit_solution(1530595403569781891)
XLA Ops:
  0.6 0.0 copy-start
  0.6 127.8 %shard_map.95 = (bf16[256,2048]{1,0:T(8,128)(2,1)}, bf16[256,2048]{1,0:T(8,128)(2,1)}, f32[1,2048]{1,0:T(1,128)}, f32[1,128]{1,0:T(1,128)}) custom-call(s32[12]{0:T(128)} %ids.1, s32[36]{0:T(128)} %sched.1, s32[9]{0:T(128)} %window.1, f32[256,2048]{1,0:T(8,128)} %bitcast.10, bf16[2048,384]{1,0:T(8,128)(2,1)} %bitcast.11, bf16[512,2048]{1,0:T(8,128)(2,1)} %ae_ref.1, ...), custom_call_target="tpu_custom_call" | custom-call | tf_op jit(solution)/shard_map/pallas_call | solution.py:395
  128.4 0.0 copy-done
  128.4 4.8 %fusion = (f32[1,256,2048]{2,1,0:T(8,128)}, f32[1,256,2048]{2,1,0:T(8,128)}) fusion(bf16[256,2048]{1,0:T(8,128)(2,1)} %get-tuple-element.9, f32[2048]{0:T(1024)} %bitcast.12, f32[]{:T(128)} %bitcast.13, bf16[256,2048]{1,0:T(8,128)(2,1)} %get-tuple-element.6, f32[1,256,2048]{2,1,0:T(8,128)S(1)} %copy-done, pred[]{:T(512)S(6)} %eq.3), kind=kLoop, calls=%fused_computation.2 | loop fusion | flops 3145728 | bytes 8396805 | tf_op jit(solution)/shard_map/broadcast_in_dim | solution.py:449
Async XLA Ops:
  0.6 127.8 %copy-start = (f32[1,256,2048]{2,1,0:T(8,128)S(1)}, f32[1,256,2048]{2,1,0:T(8,128)}, u32[]{:S(2)}) copy-start(f32[1,256,2048]{2,1,0:T(8,128)} %param.8) | copy-start | bytes 6291460

commit v3 on v2

--- a/solution.py
+++ b/solution.py
@@ -10,8 +10,10 @@
 MESH = pl.DeviceIdType.MESH
 F32, BF16 = jnp.float32, jnp.bfloat16
 PIECES = 8
+LAGS = ((3, "begin"), (5, "middle"), (7, "end"))
 PIECE = 256 // PIECES
-KEYS = 2048
+GROUPS = ((0, 1, 12, 4, 2), (3, 5, 13), (6, 8, 9), (14, 15, 7), (10, 11))
+ORDER = sum(GROUPS, ())
 FACTOR = 2.5 / math.sqrt(128) * math.log2(math.e)
 
 
@@ -28,9 +30,9 @@
 def sweep_kernel(
     ids, sched, window, x_ref, w_ref, ae_ref, md_ref, mu_ref,
     mixed, pin, gate_ref, delta_ref,
-    xbuf, wraw, wmod, bias, ae, md, mu, qkv, v1, ostage, pout, gd,
+    xbuf, wraw, wmod, bias, ae, md, mu, qk, v1, acc, ostage, pout, gd, sout, tin, in0, in1,
     load_sem, home_s, home_r, guest_s, guest_r, share_s, share_r, wx_s, wx_r,
-    hop_s, hop_r, out_s, out_r, chain_s, chain_r,
+    hop_s, hop_r, out_s, out_r, t_s, t_r, s0_s, s0_r, s1_s, s1_r, e_s, e_r,
 ):
     step, seq = lax.axis_index("step"), lax.axis_index("seq")
     y, c = step // 2, lax.rem(step, 2)
@@ -46,11 +48,10 @@
     up, down = device(c, 1, x), device(c, -1, x)
     sibling = device(1 - c, 0, x)
     across = [device(core, 0, 3 - x) for core in range(2)]
-    after = (lax.rem(step + 1, 8), seq)
-    before = (lax.rem(step + 7, 8), seq)
+    planes = [(lax.rem(y + dy, 4) * 2 + c, seq) for dy in (1, 3, 2)]
 
     barrier = pltpu.get_barrier_semaphore()
-    for other in (mate, up, down, sibling, *across, after, before):
+    for other in (mate, up, down, sibling, *across, *planes):
         pl.semaphore_signal(barrier, inc=1, device_id=other, device_id_type=MESH)
     for other_z in range(4):
         for column in range(2):
@@ -78,9 +79,6 @@
     mine = pl.ds(pl.multiple_of(c * 128, 128), 128)
     theirs = pl.ds(pl.multiple_of((1 - c) * 128, 128), 128)
 
-    value = x_ref[...]
-    unit = (value * inverse_rms(value)).astype(BF16)
-
     home_out = [
         remote(xbuf.at[0, theirs], xbuf.at[0, theirs], home_s.at[0], home_r.at[0], sibling),
         remote(xbuf.at[0, mine], xbuf.at[0, mine], home_s.at[1], home_r.at[1], sibling),
@@ -90,7 +88,20 @@
         for core in range(2)
     ]
 
-    pl.semaphore_wait(barrier, 8 + 16 - stays.astype(jnp.int32))
+    pl.semaphore_wait(barrier, 9 + 16 - stays.astype(jnp.int32))
+
+    quarter = pl.ds(pl.multiple_of(y * 512, 512), 512)
+    w_across = remote(w_ref.at[quarter], wraw.at[quarter], wx_s.at[0], wx_r.at[0], across[1])
+    w_planes = [
+        remote(wraw.at[quarter], wraw.at[quarter], wx_s.at[i + 1], wx_r.at[i + 1], planes[i]) for i in range(3)
+    ]
+
+    @pl.when(c == 1)
+    def _():
+        w_across.start()
+
+    value = x_ref[...]
+    unit = (value * inverse_rms(value)).astype(BF16)
 
     @pl.when(stays)
     def _():
@@ -159,16 +170,16 @@
     shift_high = shift.astype(BF16)
     shift_low = (shift - shift_high.astype(F32)).astype(BF16)
 
+    @pl.when(c == 1)
+    def _():
+        w_across.wait_recv()
+        for copy in w_planes:
+            copy.start()
+
     guest_out[0].wait_recv()
     g01, g30, g10 = hop(3, 1, mate, 3), hop(4, 1, up, 13), hop(5, 1, down, 5)
     for copy in (g01, g30, g10):
         copy.start()
-    w_across = remote(w_ref, wraw, wx_s, wx_r, across[1])
-
-    @pl.when(c == 1)
-    def _():
-        w_across.start()
-
     share(1)
     h30.wait_recv()
     h20, x31h = hop(6, 12, up, 8), hop(7, 12, mate, 14)
@@ -200,7 +211,8 @@
 
     @pl.when(c == 1)
     def _():
-        w_across.wait_recv()
+        for copy in w_planes:
+            copy.wait_recv()
 
     for i in range(4):
         part = pl.ds(i * 512, 512)
@@ -209,29 +221,61 @@
     shifted += jnp.dot(shift_low, wraw[...], preferred_element_type=F32)
     rows = lax.broadcasted_iota(jnp.int32, (8, 384), 0)
     bias[...] = jnp.sum(jnp.where(rows == m, shifted, 0.0), axis=0, keepdims=True)
-    v1[:, 128:] = jnp.ones((4096, 128), BF16)
-
-    def project(slot):
+    v1[:, :, 128:] = jnp.ones((16, 256, 128), BF16)
+
+    def block_of(slot):
         zr, kind = slot // 4, slot % 4
         other = x + 1 - 2 * lax.rem(x, 2)
-        column = (x, 3 - x, other, 3 - other)[kind]
-        block = lax.rem(z + zr, 4) * 4 + column
+        return lax.rem(z + zr, 4) * 4 + (x, 3 - x, other, 3 - other)[kind]
+
+    def project(slot):
+        place = ORDER.index(slot)
         p = jnp.dot(xbuf[slot], wmod[...], preferred_element_type=F32) + bias[...]
         q, k = p[:, :128], p[:, 128:256]
-        rows = pl.ds(pl.multiple_of(block * 256, 256), 256)
-        qkv[rows, :128] = (q * (inverse_rms(q) * FACTOR)).astype(BF16)
-        qkv[rows, 128:] = (k * inverse_rms(k)).astype(BF16)
-        v1[rows, :128] = p[:, 256:].astype(BF16)
-
-    @pl.when(jnp.logical_not(stays))
-    def _():
-        home_out[1].wait_recv()
-
-    project(0)
-    for slot in (1, 12, 4, 2):
-        shares[slot].wait_recv()
-        project(slot)
-
+        qk[place, :, :128] = (q * (inverse_rms(q) * FACTOR)).astype(BF16)
+        qk[place, :, 128:] = (k * inverse_rms(k)).astype(BF16)
+        v1[place, :, :128] = p[:, 256:].astype(BF16)
+
+    def weigh(q, first, last):
+        keys = qk[first:last, :, 128:].reshape((last - first) * 256, 128)
+        values = v1[first:last].reshape((last - first) * 256, 256)
+        s = lax.dot_general(q, keys, (((1,), (1,)), ((), ())), preferred_element_type=F32)
+        return jnp.dot(jnp.exp2(s).astype(BF16), values, preferred_element_type=F32)
+
+    def fresh(first, last):
+        count = last - first
+        q = qk[first:last, :, :128].reshape(count * 256, 128)
+        for at in range(0, last, 4):
+            part = weigh(q, at, min(at + 4, last)).reshape(count, 256, 256)
+            if at == 0:
+                acc[first:last] = part
+            else:
+                acc[first:last] += part
+
+    def extend(first, last):
+        for half in range(2):
+            rows = pl.ds(half * 128, 128)
+            q = qk[:first, rows, :128].reshape(first * 128, 128)
+            acc[:first, rows] += weigh(q, first, last).reshape(first, 128, 256)
+
+    def absorb(group):
+        first = ORDER.index(GROUPS[group][0])
+        last = first + len(GROUPS[group])
+        for slot in GROUPS[group]:
+            if slot:
+                shares[slot].wait_recv()
+            else:
+                @pl.when(jnp.logical_not(stays))
+                def _():
+                    home_out[1].wait_recv()
+            project(slot)
+        if group < len(GROUPS) - 1:
+            if group:
+                extend(first, last)
+            fresh(first, last)
+
+    absorb(0)
+    absorb(1)
     x11h.wait_recv()
     part11 = hop(12, 6, down, 10, 32, 32)
     part11.start()
@@ -242,9 +286,7 @@
     share(8)
     g20.wait_recv()
     share(9)
-    for slot in (3, 5, 13):
-        shares[slot].wait_recv()
-        project(slot)
+    absorb(2)
     x31h.wait_recv()
     part31 = hop(14, 14, up, 10, 0, 32)
     part31.start()
@@ -257,12 +299,7 @@
     part11g = hop(16, 7, down, 11, 64, 64)
     part11g.start()
     share(7)
-    for slot in (6, 8, 9):
-        shares[slot].wait_recv()
-        project(slot)
-    for slot in (14, 15, 7):
-        shares[slot].wait_recv()
-        project(slot)
+    absorb(3)
     part31.wait_recv()
     part11.wait_recv()
     part20.wait_recv()
@@ -270,9 +307,165 @@
     part31g.wait_recv()
     part11g.wait_recv()
     share(11)
-    for slot in (10, 11):
-        shares[slot].wait_recv()
-        project(slot)
+    absorb(4)
+    fresh(14, 16)
+
+    @pl.when(jnp.logical_not(stays))
+    def _():
+        for copy in guest_out:
+            copy.wait_send()
+
+
+    own_columns = pl.ds(pl.multiple_of(head * 128, 128), 128)
+    dests = [block_of(slot) for slot in ORDER]
+
+    def rows_of(p):
+        return pl.ds(pl.multiple_of(p * PIECE, PIECE), PIECE)
+
+    def out_copy(p, place):
+        return remote(
+            ostage.at[p, place], mixed.at[rows_of(p), own_columns], out_s, out_r.at[p], (y * 2 + m, dests[place])
+        )
+
+    def keep_copy(p):
+        return pltpu.make_async_copy(ostage.at[p, 0], mixed.at[rows_of(p), own_columns], out_r.at[p])
+
+    def finish(p):
+        rows = rows_of(p)
+        q = qk[:14, rows, :128].reshape(14 * PIECE, 128)
+        early = acc[:14, rows].reshape(14 * PIECE, 256) + weigh(q, 14, 16)
+        late = acc[14:, rows].reshape(2 * PIECE, 256)
+        ostage[p, :14] = (early[:, :128] / early[:, 128:]).astype(BF16).reshape(14, PIECE, 128)
+        ostage[p, 14:] = (late[:, :128] / late[:, 128:]).astype(BF16).reshape(2, PIECE, 128)
+
+        @pl.when(stays)
+        def _():
+            keep_copy(p).start()
+
+        @pl.when(jnp.logical_not(stays))
+        def _():
+            out_copy(p, 0).start()
+
+        for place in range(1, 16):
+            out_copy(p, place).start()
+
+    def hand(src, dst, send, recv, p, to):
+        return remote(src.at[rows_of(p)], dst.at[rows_of(p)], send.at[p], recv.at[p], to)
+
+    above, below, _ = planes
+    term_copy = lambda p: hand(pout, tin, t_s, t_r, p, sibling)
+    sum_up = lambda p: hand(sout, in0, s0_s, s0_r, p, above)
+    sum_wrap = lambda p: hand(sout, in0, s1_s, s0_r, p, below)
+    sum_next = lambda p: hand(sout, in1, s1_s, s1_r, p, above)
+    pass_down = lambda p: hand(in0, in0, s0_s, s0_r, p, below)
+    back_in0 = lambda p: hand(in0, pin, e_s, e_r, p, sibling)
+    back_pout = lambda p: hand(pout, pin, e_s, e_r, p, sibling)
+
+    def load(ref, p):
+        return ref[rows_of(p)].astype(F32)
+
+    def begin(p):
+        rows = rows_of(p)
+        pltpu.make_async_copy(mixed.at[rows], mixed.at[rows], out_r.at[p]).wait()
+        term = gd[...] * load(mixed, p)
+
+        @pl.when(c == 0)
+        def _():
+            @pl.when(y == 0)
+            def _():
+                pout[rows] = (x_ref[rows] + term).astype(BF16)
+
+            @pl.when(y > 0)
+            def _():
+                pout[rows] = term.astype(BF16)
+
+            term_copy(p).start()
+
+        @pl.when(c == 1)
+        def _():
+            term_copy(p).wait_recv()
+
+            @pl.when(y < 2)
+            def _():
+                sout[rows] = (load(tin, p) + term).astype(BF16)
+
+            @pl.when(y == 0)
+            def _():
+                sum_up(p).start()
+                sum_wrap(p).start()
+
+            @pl.when(y == 1)
+            def _():
+                sum_next(p).start()
+
+            @pl.when(y == 2)
+            def _():
+                sout[rows] = (load(tin, p) + term).astype(BF16)
+
+    def middle(p):
+        rows = rows_of(p)
+
+        @pl.when(jnp.logical_and(c == 1, y == 2))
+        def _():
+            sum_next(p).wait_recv()
+            sout[rows] = (load(in1, p) + load(sout, p)).astype(BF16)
+            sum_next(p).start()
+
+        @pl.when(jnp.logical_and(c == 1, y == 3))
+        def _():
+            sum_up(p).wait_recv()
+            pass_down(p).start()
+
+    def end(p):
+        rows = rows_of(p)
+
+        @pl.when(jnp.logical_and(c == 0, y > 0))
+        def _():
+            back_in0(p).wait_recv()
+
+        @pl.when(jnp.logical_and(c == 1, y == 0))
+        def _():
+            pin[rows] = tin[rows]
+
+        @pl.when(jnp.logical_and(c == 1, y == 1))
+        def _():
+            sum_up(p).wait_recv()
+            back_in0(p).start()
+            pin[rows] = (load(in0, p) + load(tin, p)).astype(BF16)
+
+        @pl.when(jnp.logical_and(c == 1, y > 1))
+        def _():
+            @pl.when(y == 2)
+            def _():
+                pass_down(p).wait_recv()
+
+            @pl.when(y == 3)
+            def _():
+                sum_next(p).wait_recv()
+
+            total = load(in0, p) + load(in1, p)
+            pout[rows] = total.astype(BF16)
+            back_pout(p).start()
+            pin[rows] = (total + load(tin, p)).astype(BF16)
+
+    def body(p, carry):
+        @pl.when(p < PIECES)
+        def _():
+            finish(p)
+
+        for lag, part in LAGS:
+            @pl.when(jnp.logical_and(p >= lag, p < PIECES + lag))
+            def _(lag=lag, part=part):
+                stages[part](p - lag)
+        return carry
+
+    stages = {"begin": begin, "middle": middle, "end": end}
+    lax.fori_loop(0, PIECES + LAGS[-1][0], body, 0)
+
+    @pl.when(step == 0)
+    def _():
+        pin[...] = jnp.zeros_like(pin)
+
     for copy in hops:
         copy.wait_send()
     for slot in shares:
@@ -282,106 +475,41 @@
     def _():
         for copy in home_out:
             copy.wait_send()
+        pltpu.make_async_copy(ostage.at[:, 1:], ostage.at[:, 1:], out_s).wait()
 
     @pl.when(jnp.logical_not(stays))
     def _():
-        for copy in guest_out:
+        pltpu.make_async_copy(ostage, ostage, out_s).wait()
+
+    @pl.when(c == 1)
+    def _():
+        w_across.wait_send()
+        for copy in w_planes:
             copy.wait_send()
 
-    @pl.when(c == 1)
-    def _():
-        w_across.wait_send()
-
-    own_columns = pl.ds(pl.multiple_of(head * 128, 128), 128)
-
-    def rows_of(p):
-        return pl.ds(pl.multiple_of(p * PIECE, PIECE), PIECE)
-
-    def out_copy(p, o):
-        to = lax.rem(seq + o, 16)
-        return remote(
-            ostage.at[p, to], mixed.at[rows_of(p), own_columns], out_s.at[p, o], out_r.at[p, head], (y * 2 + m, to)
-        )
-
-    def keep_copy(p):
-        return pltpu.make_async_copy(ostage.at[p, seq], mixed.at[rows_of(p), own_columns], out_r.at[p, head])
-
-    def arrival(p, other):
-        columns = pl.ds(other * 128, 128)
-        return pltpu.make_async_copy(ostage.at[p, 0], mixed.at[rows_of(p), columns], out_r.at[p, other])
-
-    def chain_copy(p):
-        return remote(pout.at[rows_of(p)], pin.at[rows_of(p)], chain_s.at[p], chain_r.at[p], after)
-
-    def attend(p):
-        q = jnp.concatenate(
-            [qkv[pl.ds(pl.multiple_of(s * 256 + p * PIECE, PIECE), PIECE), :128] for s in range(16)], axis=0
-        )
-        acc = jnp.zeros((16 * PIECE, 256), F32)
-        for j in range(0, 4096, KEYS):
-            s = lax.dot_general(
-                q, qkv[j:j + KEYS, 128:], (((1,), (1,)), ((), ())), preferred_element_type=F32
-            )
-            acc += jnp.dot(jnp.exp2(s).astype(BF16), v1[j:j + KEYS], preferred_element_type=F32)
-        o = (acc[:, :128] / acc[:, 128:]).astype(BF16)
-        for s in range(16):
-            ostage[p, s] = o[s * PIECE:(s + 1) * PIECE]
-
-        @pl.when(stays)
-        def _():
-            keep_copy(p).start()
-
-        @pl.when(jnp.logical_not(stays))
-        def _():
-            out_copy(p, 0).start()
-
-        for o in range(1, 16):
-            out_copy(p, o).start()
-
-    def chain(p):
-        rows = rows_of(p)
-        for other in range(16):
-            arrival(p, other).wait()
-
-        @pl.when(step == 0)
-        def _():
-            pout[rows] = (x_ref[rows] + gd[...] * mixed[rows].astype(F32)).astype(BF16)
-
-        @pl.when(step > 0)
-        def _():
-            chain_copy(p).wait_recv()
-            pout[rows] = (pin[rows].astype(F32) + gd[...] * mixed[rows].astype(F32)).astype(BF16)
-
-        @pl.when(step < 7)
-        def _():
-            chain_copy(p).start()
-
-    def body(p, carry):
-        attend(p)
-
-        @pl.when(p > 0)
-        def _():
-            chain(p - 1)
-        return carry
-
-    lax.fori_loop(0, PIECES, body, 0)
-    chain(PIECES - 1)
-
-    @pl.when(step == 0)
-    def _():
-        pin[...] = jnp.zeros_like(pin)
-
     def drain(p, carry):
-        @pl.when(jnp.logical_not(stays))
-        def _():
-            out_copy(p, 0).wait_send()
-
-        for o in range(1, 16):
-            out_copy(p, o).wait_send()
-
-        @pl.when(step < 7)
-        def _():
-            chain_copy(p).wait_send()
+        @pl.when(c == 0)
+        def _():
+            term_copy(p).wait_send()
+
+        @pl.when(c == 1)
+        def _():
+            @pl.when(y == 0)
+            def _():
+                sum_up(p).wait_send()
+                sum_wrap(p).wait_send()
+
+            @pl.when(jnp.logical_or(y == 1, y == 2))
+            def _():
+                sum_next(p).wait_send()
+
+            @pl.when(y == 3)
+            def _():
+                pass_down(p).wait_send()
+
+            @pl.when(y > 0)
+            def _():
+                back_in0(p).wait_send()
         return carry
 
     lax.fori_loop(0, PIECES, drain, 0)
@@ -408,13 +536,19 @@
             pltpu.VMEM((512, 2048), BF16),
             pltpu.VMEM((2048, 256), BF16),
             pltpu.VMEM((256, 6144), BF16),
-            pltpu.VMEM((4096, 256), BF16),
-            pltpu.VMEM((4096, 256), BF16),
+            pltpu.VMEM((16, 256, 256), BF16),
+            pltpu.VMEM((16, 256, 256), BF16),
+            pltpu.VMEM((16, 256, 256), F32),
             pltpu.VMEM((PIECES, 16, PIECE, 128), BF16),
             pltpu.VMEM((256, 2048), BF16),
             pltpu.VMEM((1, 2048), F32),
-            dma((4,)), dma((2,)), dma((2,)), dma((2,)), dma, dma((16,)), dma((16,)), dma, dma,
-            dma((17,)), dma((17,)), dma((PIECES, 16)), dma((PIECES, 16)), dma((PIECES,)), dma((PIECES,)),
+            pltpu.VMEM((256, 2048), BF16),
+            pltpu.VMEM((256, 2048), BF16),
+            pltpu.VMEM((256, 2048), BF16),
+            pltpu.VMEM((256, 2048), BF16),
+            dma((4,)), dma((2,)), dma((2,)), dma((2,)), dma, dma((16,)), dma((16,)), dma((4,)), dma((4,)),
+            dma((17,)), dma((17,)), dma, dma((PIECES,)),
+            *[dma((PIECES,)) for _ in range(8)],
         ],
         compiler_params=pltpu.CompilerParams(
             collective_id=1, has_side_effects=True, vmem_limit_bytes=60 * 1024 * 1024

time: 133 us -> 120 us (0.902)
  Pallas kernels: 128 us -> 114 us
    pallas_call x1, Pallas kernels: 128 us -> 114 us  [sweep(): pl.pallas_call(sweep_kernel, out_shape=(jax.ShapeDtypeStruct((256, 2048),...]
where the time goes in v3:
time: 120 us
  Pallas kernels  114 us (95%)
  other arithmetic  4.79 us (4%)
    pallas_call x1, Pallas kernels, sweep(): pl.pallas_call(sweep_kernel, out_shape=(jax.ShapeDtypeStruct((256, 2048),...  114 us
    broadcast_in_dim x1, other arithmetic, on_device(): return (new_states[None], velocity[None])  4.79 us

profile of v3, /device:TPU:25, one launch (start us, length us, event | category | flops | bytes accessed | tf_op | source)
XLA Modules:
  0.0 119.6 jit_solution(9733656669817715702)
XLA Ops:
  0.6 0.0 copy-start
  0.6 114.2 %shard_map.95 = (bf16[256,2048]{1,0:T(8,128)(2,1)}, bf16[256,2048]{1,0:T(8,128)(2,1)}, f32[1,2048]{1,0:T(1,128)}, f32[1,128]{1,0:T(1,128)}) custom-call(s32[12]{0:T(128)} %ids.1, s32[36]{0:T(128)} %sched.1, s32[9]{0:T(128)} %window.1, f32[256,2048]{1,0:T(8,128)} %bitcast.10, bf16[2048,384]{1,0:T(8,128)(2,1)} %bitcast.11, bf16[512,2048]{1,0:T(8,128)(2,1)} %ae_ref.1, ...), custom_call_target="tpu_custom_call" | custom-call | tf_op jit(solution)/shard_map/pallas_call | solution.py:523
  114.8 0.0 copy-done
  114.8 4.8 %fusion = (f32[1,256,2048]{2,1,0:T(8,128)}, f32[1,256,2048]{2,1,0:T(8,128)}) fusion(bf16[256,2048]{1,0:T(8,128)(2,1)} %get-tuple-element.9, f32[2048]{0:T(1024)} %bitcast.12, f32[]{:T(128)} %bitcast.13, bf16[256,2048]{1,0:T(8,128)(2,1)} %get-tuple-element.6, f32[1,256,2048]{2,1,0:T(8,128)S(1)} %copy-done, pred[]{:T(512)S(6)} %eq.3), kind=kLoop, calls=%fused_computation.2 | loop fusion | flops 3145728 | bytes 8396805 | tf_op jit(solution)/shard_map/broadcast_in_dim | solution.py:583
Async XLA Ops:
  0.6 114.2 %copy-start = (f32[1,256,2048]{2,1,0:T(8,128)S(1)}, f32[1,256,2048]{2,1,0:T(8,128)}, u32[]{:S(2)}) copy-start(f32[1,256,2048]{2,1,0:T(8,128)} %param.8) | copy-start | bytes 6291460

commit v4 on v3

--- a/solution.py
+++ b/solution.py
@@ -10,6 +10,7 @@
 MESH = pl.DeviceIdType.MESH
 F32, BF16 = jnp.float32, jnp.bfloat16
 PIECES = 8
+REST = ((0, 8, 8), (8, 11, 11), (11, 14, 14), (14, 16, 16))
 LAGS = ((3, "begin"), (5, "middle"), (7, "end"))
 PIECE = 256 // PIECES
 GROUPS = ((0, 1, 12, 4, 2), (3, 5, 13), (6, 8, 9), (14, 15, 7), (10, 11))
@@ -28,11 +29,12 @@
 
 
 def sweep_kernel(
-    ids, sched, window, x_ref, w_ref, ae_ref, md_ref, mu_ref,
-    mixed, pin, gate_ref, delta_ref,
+    ids, sched, window, x_hbm, w_ref, ae_ref, md_ref, mu_ref,
+    new_ref, vel_ref,
+    mixed, pin, new, vel, x_ref, gate_row,
     xbuf, wraw, wmod, bias, ae, md, mu, qk, v1, acc, ostage, pout, gd, sout, tin, in0, in1,
     load_sem, home_s, home_r, guest_s, guest_r, share_s, share_r, wx_s, wx_r,
-    hop_s, hop_r, out_s, out_r, t_s, t_r, s0_s, s0_r, s1_s, s1_r, e_s, e_r,
+    hop_s, hop_r, out_s, out_r, t_s, t_r, s0_s, s0_r, s1_s, s1_r, e_s, e_r, put_sem,
 ):
     step, seq = lax.axis_index("step"), lax.axis_index("seq")
     y, c = step // 2, lax.rem(step, 2)
@@ -44,6 +46,8 @@
     def device(core, dz, column):
         return (y * 2 + core, lax.rem(z + dz + 4, 4) * 4 + column)
 
+    x_load = pltpu.make_async_copy(x_hbm, x_ref, load_sem.at[4])
+    x_load.start()
     mate = device(c, 0, x + 1 - 2 * lax.rem(x, 2))
     up, down = device(c, 1, x), device(c, -1, x)
     sibling = device(1 - c, 0, x)
@@ -100,6 +104,7 @@
     def _():
         w_across.start()
 
+    x_load.wait()
     value = x_ref[...]
     unit = (value * inverse_rms(value)).astype(BF16)
 
@@ -161,8 +166,7 @@
     rows = lax.broadcasted_iota(jnp.int32, (8, 2048), 0)
     gate = jnp.sum(jnp.where(rows == c, factors[:, 4096:], 0.0), axis=0, keepdims=True)
     delta = jnp.where(c == 0, stamps[1] / 1000.0 - stamps[0] / 1000.0, stamps[2] / 1000.0 - stamps[1] / 1000.0)
-    gate_ref[...] = gate
-    delta_ref[...] = jnp.full((1, 128), delta, F32)
+    gate_row[...] = gate
     gd[...] = gate * delta
     columns = lax.broadcasted_iota(jnp.int32, (2048, 8), 1)
     scale = jnp.sum(jnp.where(columns == m, scale_cols, 0.0), axis=1, keepdims=True)
@@ -269,10 +273,9 @@
                 def _():
                     home_out[1].wait_recv()
             project(slot)
-        if group < len(GROUPS) - 1:
-            if group:
-                extend(first, last)
-            fresh(first, last)
+        if 0 < group < 2:
+            extend(first, last)
+        fresh(first, last)
 
     absorb(0)
     absorb(1)
@@ -286,7 +289,6 @@
     share(8)
     g20.wait_recv()
     share(9)
-    absorb(2)
     x31h.wait_recv()
     part31 = hop(14, 14, up, 10, 0, 32)
     part31.start()
@@ -299,6 +301,7 @@
     part11g = hop(16, 7, down, 11, 64, 64)
     part11g.start()
     share(7)
+    absorb(2)
     absorb(3)
     part31.wait_recv()
     part11.wait_recv()
@@ -308,7 +311,6 @@
     part11g.wait_recv()
     share(11)
     absorb(4)
-    fresh(14, 16)
 
     @pl.when(jnp.logical_not(stays))
     def _():
@@ -332,11 +334,13 @@
 
     def finish(p):
         rows = rows_of(p)
-        q = qk[:14, rows, :128].reshape(14 * PIECE, 128)
-        early = acc[:14, rows].reshape(14 * PIECE, 256) + weigh(q, 14, 16)
-        late = acc[14:, rows].reshape(2 * PIECE, 256)
-        ostage[p, :14] = (early[:, :128] / early[:, 128:]).astype(BF16).reshape(14, PIECE, 128)
-        ostage[p, 14:] = (late[:, :128] / late[:, 128:]).astype(BF16).reshape(2, PIECE, 128)
+        for first, last, done in REST:
+            count = last - first
+            total = acc[first:last, rows].reshape(count * PIECE, 256)
+            q = qk[first:last, rows, :128].reshape(count * PIECE, 128)
+            for at in range(done, 16, 4):
+                total += weigh(q, at, min(at + 4, 16))
+            ostage[p, first:last] = (total[:, :128] / total[:, 128:]).astype(BF16).reshape(count, PIECE, 128)
 
         @pl.when(stays)
         def _():
@@ -367,7 +371,10 @@
     def begin(p):
         rows = rows_of(p)
         pltpu.make_async_copy(mixed.at[rows], mixed.at[rows], out_r.at[p]).wait()
-        term = gd[...] * load(mixed, p)
+        here = load(mixed, p)
+        term = gd[...] * here
+        vel[rows] = gate_row[...] * here
+        pltpu.make_async_copy(vel.at[rows], vel_ref.at[rows], put_sem.at[0]).start()
 
         @pl.when(c == 0)
         def _():
@@ -419,19 +426,26 @@
     def end(p):
         rows = rows_of(p)
 
+        term = gd[...] * load(mixed, p)
+
+        @pl.when(step == 0)
+        def _():
+            new[rows] = x_ref[rows] + term
+
         @pl.when(jnp.logical_and(c == 0, y > 0))
         def _():
             back_in0(p).wait_recv()
+            new[rows] = load(pin, p) + term
 
         @pl.when(jnp.logical_and(c == 1, y == 0))
         def _():
-            pin[rows] = tin[rows]
+            new[rows] = load(tin, p) + term
 
         @pl.when(jnp.logical_and(c == 1, y == 1))
         def _():
             sum_up(p).wait_recv()
             back_in0(p).start()
-            pin[rows] = (load(in0, p) + load(tin, p)).astype(BF16)
+            new[rows] = load(in0, p) + load(tin, p) + term
 
         @pl.when(jnp.logical_and(c == 1, y > 1))
         def _():
@@ -446,7 +460,9 @@
             total = load(in0, p) + load(in1, p)
             pout[rows] = total.astype(BF16)
             back_pout(p).start()
-            pin[rows] = (total + load(tin, p)).astype(BF16)
+            new[rows] = total + load(tin, p) + term
+
+        pltpu.make_async_copy(new.at[rows], new_ref.at[rows], put_sem.at[1]).start()
 
     def body(p, carry):
         @pl.when(p < PIECES)
@@ -462,10 +478,6 @@
     stages = {"begin": begin, "middle": middle, "end": end}
     lax.fori_loop(0, PIECES + LAGS[-1][0], body, 0)
 
-    @pl.when(step == 0)
-    def _():
-        pin[...] = jnp.zeros_like(pin)
-
     for copy in hops:
         copy.wait_send()
     for slot in shares:
@@ -513,22 +525,28 @@
         return carry
 
     lax.fori_loop(0, PIECES, drain, 0)
+    pltpu.make_async_copy(vel, vel_ref, put_sem.at[0]).wait()
+    pltpu.make_async_copy(new, new_ref, put_sem.at[1]).wait()
 
 
 def sweep(ids, sched, window, x, w, ae, md, mu):
-    vm = pl.BlockSpec(memory_space=pltpu.VMEM)
     sm = pl.BlockSpec(memory_space=pltpu.SMEM)
     anywhere = pl.BlockSpec(memory_space=pl.ANY)
     dma = pltpu.SemaphoreType.DMA
     return pl.pallas_call(
         sweep_kernel,
         out_shape=(
-            jax.ShapeDtypeStruct((256, 2048), BF16), jax.ShapeDtypeStruct((256, 2048), BF16),
-            jax.ShapeDtypeStruct((1, 2048), F32), jax.ShapeDtypeStruct((1, 128), F32),
+            jax.ShapeDtypeStruct((256, 2048), F32), jax.ShapeDtypeStruct((256, 2048), F32),
         ),
-        in_specs=[sm, sm, sm, vm, anywhere, anywhere, anywhere, anywhere],
-        out_specs=(vm, vm, vm, vm),
+        in_specs=[sm, sm, sm, anywhere, anywhere, anywhere, anywhere, anywhere],
+        out_specs=(anywhere, anywhere),
         scratch_shapes=[
+            pltpu.VMEM((256, 2048), BF16),
+            pltpu.VMEM((256, 2048), BF16),
+            pltpu.VMEM((256, 2048), F32),
+            pltpu.VMEM((256, 2048), F32),
+            pltpu.VMEM((256, 2048), F32),
+            pltpu.VMEM((1, 2048), F32),
             pltpu.VMEM((16, 256, 2048), BF16),
             pltpu.VMEM((2048, 384), BF16),
             pltpu.VMEM((2048, 384), BF16),
@@ -546,9 +564,9 @@
             pltpu.VMEM((256, 2048), BF16),
             pltpu.VMEM((256, 2048), BF16),
             pltpu.VMEM((256, 2048), BF16),
-            dma((4,)), dma((2,)), dma((2,)), dma((2,)), dma, dma((16,)), dma((16,)), dma((4,)), dma((4,)),
+            dma((5,)), dma((2,)), dma((2,)), dma((2,)), dma, dma((16,)), dma((16,)), dma((4,)), dma((4,)),
             dma((17,)), dma((17,)), dma, dma((PIECES,)),
-            *[dma((PIECES,)) for _ in range(8)],
+            *[dma((PIECES,)) for _ in range(8)], dma((2,)),
         ],
         compiler_params=pltpu.CompilerParams(
             collective_id=1, has_side_effects=True, vmem_limit_bytes=60 * 1024 * 1024
@@ -566,20 +584,16 @@
     sched,
     window,
 ):
-    rows = iterate[0]
-    mixed, earlier, gate, delta = sweep(
+    new_states, velocity = sweep(
         action_token_index,
         sched,
         window,
-        rows,
+        iterate[0],
         query_key_value_weight[:, 0],
         action_embedding_matrix,
         modulation_down_weight,
         modulation_up_weight,
     )
-    velocity = gate * mixed.astype(F32)
-    entering = jnp.where(lax.axis_index("step") == 0, rows, earlier.astype(F32))
-    new_states = entering + delta[:, :1] * velocity
     return (new_states[None], velocity[None])
 
 

time: 120 us -> 113 us (0.942)
  Pallas kernels: 114 us -> 107 us
  other arithmetic: 4.79 us -> 0 us
  local copies, waits for them, and re-layouts: 0.01 us -> 4.61 us
    pallas_call x1, Pallas kernels: 114 us -> 107 us  [sweep(): pl.pallas_call(sweep_kernel, out_shape=(jax.ShapeDtypeStruct((256, 2048),...]
    broadcast_in_dim x1 -> x0, other arithmetic: 4.79 us -> none  [on_device(): return (new_states[None], velocity[None])]
    unnamed x2 -> x4, local copies, waits for them, and re-layouts: 0.01 us -> 4.61 us
where the time goes in v4:
time: 113 us; the launch traced here: 112 us
  Pallas kernels  107 us (95%)
  local copies, waits for them, and re-layouts  4.61 us (4%)
    pallas_call x1, Pallas kernels, sweep(): pl.pallas_call(sweep_kernel, out_shape=(jax.ShapeDtypeStruct((256, 2048),...  107 us
    unnamed x4, local copies, waits for them, and re-layouts  4.61 us

profile of v4, /device:TPU:25, one launch (start us, length us, event | category | flops | bytes accessed | tf_op | source)
XLA Modules:
  0.0 112.1 jit_solution(10927811481102627344)
XLA Ops:
  0.6 106.8 %shard_map.95 = (f32[256,2048]{1,0:T(8,128)}, f32[256,2048]{1,0:T(8,128)}) custom-call(s32[12]{0:T(128)} %ids.1, s32[36]{0:T(128)} %sched.1, s32[9]{0:T(128)} %window.1, f32[256,2048]{1,0:T(8,128)} %bitcast.6, bf16[2048,384]{1,0:T(8,128)(2,1)} %bitcast.7, bf16[512,2048]{1,0:T(8,128)(2,1)} %ae_ref.1, bf16[2048,256]{1,0:T(8,128)(2,1)} %md_ref.1, ...), custom_call_target="tpu_custom_call" | custom-call | tf_op jit(solution)/shard_map/pallas_call | solution.py:536
  107.5 0.0 copy-start
  107.5 3.3 %copy.12 = f32[1,256,2048]{2,1,0:T(8,128)} copy(f32[1,256,2048]{2,1,0:T(8,128)} %bitcast.5) | data formatting | bytes 4194304
  110.8 0.0 copy-done
  110.8 1.3 %copy.13 = f32[1,256,2048]{2,1,0:T(8,128)} copy(f32[1,256,2048]{2,1,0:T(8,128)S(1)} %bitcast.4) | data formatting | bytes 4194304
Async XLA Ops:
  107.5 3.3 %copy-start = (f32[256,2048]{1,0:T(8,128)S(1)}, f32[256,2048]{1,0:T(8,128)}, u32[]{:S(2)}) copy-start(f32[256,2048]{1,0:T(8,128)} %get-tuple-element.5) | copy-start | bytes 6291460

commit v5 on v4

--- a/solution.py
+++ b/solution.py
@@ -10,7 +10,7 @@
 MESH = pl.DeviceIdType.MESH
 F32, BF16 = jnp.float32, jnp.bfloat16
 PIECES = 8
-REST = ((0, 8, 8), (8, 11, 11), (11, 14, 14), (14, 16, 16))
+REST = ((0, 16, 8),)
 LAGS = ((3, "begin"), (5, "middle"), (7, "end"))
 PIECE = 256 // PIECES
 GROUPS = ((0, 1, 12, 4, 2), (3, 5, 13), (6, 8, 9), (14, 15, 7), (10, 11))
@@ -249,7 +249,7 @@
     def fresh(first, last):
         count = last - first
         q = qk[first:last, :, :128].reshape(count * 256, 128)
-        for at in range(0, last, 4):
+        for at in range(0, min(last, 8), 4):
             part = weigh(q, at, min(at + 4, last)).reshape(count, 256, 256)
             if at == 0:
                 acc[first:last] = part
@@ -350,8 +350,15 @@
         def _():
             out_copy(p, 0).start()
 
-        for place in range(1, 16):
-            out_copy(p, place).start()
+        @pl.when(c == 0)
+        def _():
+            for place in range(1, 16):
+                out_copy(p, place).start()
+
+        @pl.when(c == 1)
+        def _():
+            for place in range(15, 0, -1):
+                out_copy(p, place).start()
 
     def hand(src, dst, send, recv, p, to):
         return remote(src.at[rows_of(p)], dst.at[rows_of(p)], send.at[p], recv.at[p], to)

time: 113 us -> 110 us (0.973)
  Pallas kernels: 107 us -> 104 us
    pallas_call x1, Pallas kernels: 107 us -> 104 us  [sweep(): pl.pallas_call(sweep_kernel, out_shape=(jax.ShapeDtypeStruct((256, 2048),...]
where the time goes in v5:
time: 110 us; the launch traced here: 109 us
  Pallas kernels  104 us (95%)
  local copies, waits for them, and re-layouts  4.61 us (4%)
    pallas_call x1, Pallas kernels, sweep(): pl.pallas_call(sweep_kernel, out_shape=(jax.ShapeDtypeStruct((256, 2048),...  104 us
    unnamed x4, local copies, waits for them, and re-layouts  4.61 us

profile of v5, /device:TPU:25, one launch (start us, length us, event | category | flops | bytes accessed | tf_op | source)
XLA Modules:
  0.0 109.1 jit_solution(16862953124304273795)
XLA Ops:
  0.6 103.8 %shard_map.95 = (f32[256,2048]{1,0:T(8,128)}, f32[256,2048]{1,0:T(8,128)}) custom-call(s32[12]{0:T(128)} %ids.1, s32[36]{0:T(128)} %sched.1, s32[9]{0:T(128)} %window.1, f32[256,2048]{1,0:T(8,128)} %bitcast.6, bf16[2048,384]{1,0:T(8,128)(2,1)} %bitcast.7, bf16[512,2048]{1,0:T(8,128)(2,1)} %ae_ref.1, bf16[2048,256]{1,0:T(8,128)(2,1)} %md_ref.1, ...), custom_call_target="tpu_custom_call" | custom-call | tf_op jit(solution)/shard_map/pallas_call | solution.py:543
  104.5 0.0 copy-start
  104.5 3.3 %copy.12 = f32[1,256,2048]{2,1,0:T(8,128)} copy(f32[1,256,2048]{2,1,0:T(8,128)} %bitcast.5) | data formatting | bytes 4194304
  107.8 0.0 copy-done
  107.8 1.3 %copy.13 = f32[1,256,2048]{2,1,0:T(8,128)} copy(f32[1,256,2048]{2,1,0:T(8,128)S(1)} %bitcast.4) | data formatting | bytes 4194304
Async XLA Ops:
  104.5 3.3 %copy-start = (f32[256,2048]{1,0:T(8,128)S(1)}, f32[256,2048]{1,0:T(8,128)}, u32[]{:S(2)}) copy-start(f32[256,2048]{1,0:T(8,128)} %get-tuple-element.5) | copy-start | bytes 6291460

commit v6 on v5

--- a/solution.py
+++ b/solution.py
@@ -105,19 +105,23 @@
         w_across.start()
 
     x_load.wait()
-    value = x_ref[...]
-    unit = (value * inverse_rms(value)).astype(BF16)
+
+    def unit(rows):
+        value = x_ref[rows]
+        return (value * inverse_rms(value)).astype(BF16)
+
 
     @pl.when(stays)
     def _():
-        xbuf[0] = unit
+        xbuf[0, theirs] = unit(theirs)
         home_out[0].start()
+        xbuf[0, mine] = unit(mine)
 
     @pl.when(jnp.logical_not(stays))
     def _():
-        pout[...] = unit
-        for copy in guest_out:
-            copy.start()
+        for core in range(2):
+            pout[core * 128:(core + 1) * 128] = unit(pl.ds(core * 128, 128))
+            guest_out[core].start()
         home_out[0].wait_recv()
 
     hops = []

time: 110 us -> 110 us (level)
  no operation moved by 1% of the time
where the time goes in v6:
time: 110 us; the launch traced here: 109 us
  Pallas kernels  104 us (95%)
  local copies, waits for them, and re-layouts  4.61 us (4%)
    pallas_call x1, Pallas kernels, sweep(): pl.pallas_call(sweep_kernel, out_shape=(jax.ShapeDtypeStruct((256, 2048),...  104 us
    unnamed x4, local copies, waits for them, and re-layouts  4.61 us

profile of v6, /device:TPU:25, one launch (start us, length us, event | category | flops | bytes accessed | tf_op | source)
XLA Modules:
  0.0 109.0 jit_solution(15863981669627501560)
XLA Ops:
  0.6 103.8 %shard_map.95 = (f32[256,2048]{1,0:T(8,128)}, f32[256,2048]{1,0:T(8,128)}) custom-call(s32[12]{0:T(128)} %ids.1, s32[36]{0:T(128)} %sched.1, s32[9]{0:T(128)} %window.1, f32[256,2048]{1,0:T(8,128)} %bitcast.6, bf16[2048,384]{1,0:T(8,128)(2,1)} %bitcast.7, bf16[512,2048]{1,0:T(8,128)(2,1)} %ae_ref.1, bf16[2048,256]{1,0:T(8,128)(2,1)} %md_ref.1, ...), custom_call_target="tpu_custom_call" | custom-call | tf_op jit(solution)/shard_map/pallas_call | solution.py:547
  104.4 0.0 copy-start
  104.4 3.3 %copy.12 = f32[1,256,2048]{2,1,0:T(8,128)} copy(f32[1,256,2048]{2,1,0:T(8,128)} %bitcast.5) | data formatting | bytes 4194304
  107.7 0.0 copy-done
  107.7 1.3 %copy.13 = f32[1,256,2048]{2,1,0:T(8,128)} copy(f32[1,256,2048]{2,1,0:T(8,128)S(1)} %bitcast.4) | data formatting | bytes 4194304
Async XLA Ops:
  104.4 3.3 %copy-start = (f32[256,2048]{1,0:T(8,128)S(1)}, f32[256,2048]{1,0:T(8,128)}, u32[]{:S(2)}) copy-start(f32[256,2048]{1,0:T(8,128)} %get-tuple-element.5) | copy-start | bytes 6291460
